TPU v7x, 32 devices: a whole 2x2x4 slice. The times are simulated.
32 devices in a mesh: grp: 2 (over y), blk: 16 (over z, x, core).
Axes of the slice: x: 2, y: 2, z: 4, core: 2. Of those that a mesh axis runs over, the one named last changes fastest.
Arguments:
- images: bfloat16 [1024, 1152], P(('blk', 'grp')), may hold values from -6 to 6
- texts: bfloat16 [1024, 1152], P(('blk', 'grp')), may hold values from -6 to 6
- tile_mask: int32 [8, 8], replicated, may hold values from 0 to 1, as said below
Outputs:
- image_grads: float32 [1024, 1152], P(('blk', 'grp'))
- text_grads: float32 [1024, 1152], P(('blk', 'grp'))
- loss_mean: float32 [], replicated
Inputs may be any that keep to these rules, and one draw needn't show every extreme that they name: tile_mask is symmetric and 1 on its diagonal.
All inputs are finite; a program needn't handle non-finite values.
Results may differ from a plain program's by a relative error of at most 0.00045.
The roundings to bfloat16 on the way count: a program that leaves them out, or rounds other values in their place, can miss the bound.
Values may be sent and summed in bfloat16 or wider, within the bound.
A program may use at most 64 MiB of HBM per device.

v0:
```python
import jax
import jax.numpy as jnp
from jax import lax
from jax.sharding import PartitionSpec as P

TILE = 128


TEMP = 10.0
BIAS = -2.0
EPS = 1e-06


def shifted(value, axis, steps):
    count = lax.axis_size(axis)
    pairs = [(source, (source + steps) % count) for source in range(count)]
    return lax.ppermute(value, axis, pairs)


def normalize(values):
    return values * lax.rsqrt(jnp.sum(values * values, axis=-1, keepdims=True) + EPS)


def tile_onehot(ids, total_tiles):
    return ((ids // TILE)[:, None] == jnp.arange(total_tiles, dtype=jnp.int32)[None, :]).astype(
        jnp.float32
    )


def on_device(images, texts, tile_mask):
    groups = lax.axis_size("grp")
    loops = lax.axis_size("blk")
    own_group = lax.axis_index("grp")
    own_place = lax.axis_index("blk")
    rows = images.shape[0]
    width = images.shape[1]
    total_tiles = tile_mask.shape[0]
    image_unit, image_back = jax.vjp(normalize, images.astype(jnp.float32))
    text_unit, text_back = jax.vjp(normalize, texts.astype(jnp.float32))
    image_bf = image_unit.astype(jnp.bfloat16)
    text_bf = text_unit.astype(jnp.bfloat16)
    gathered = lax.all_gather(image_bf, "grp", axis=0, tiled=True)
    group_rows = gathered.shape[0]
    image_ids = own_place * group_rows + jnp.arange(group_rows, dtype=jnp.int32)
    row_masks = jnp.dot(
        tile_onehot(image_ids, total_tiles),
        tile_mask.astype(jnp.float32),
        precision=lax.Precision.HIGHEST,
    )

    def ids_of(source, offset, count):
        return (source * groups + own_group) * rows + offset + jnp.arange(count, dtype=jnp.int32)

    def block_terms(block, text_ids):
        masked = jnp.dot(
            row_masks, tile_onehot(text_ids, total_tiles).T, precision=lax.Precision.HIGHEST
        )
        matched = image_ids[:, None] == text_ids[None, :]
        valid = (masked < 0.5) | matched
        count = jnp.sum(valid.astype(jnp.float32))
        logits = (
            TEMP
            * lax.dot_general(
                gathered, block, (((1,), (1,)), ((), ())), preferred_element_type=jnp.float32
            )
            + BIAS
        )
        signs = jnp.where(matched, 1.0, -1.0)
        loss = jnp.sum(jnp.where(valid, jax.nn.softplus(-signs * logits), 0.0))
        coef = jnp.where(valid, jax.nn.sigmoid(logits) - matched.astype(jnp.float32), 0.0).astype(
            jnp.bfloat16
        )
        contrib = lax.dot_general(
            coef, gathered, (((0,), (0,)), ((), ())), preferred_element_type=jnp.float32
        )
        coef, contrib, loss = (coef, contrib, loss)
        return (coef, contrib, loss, count)

    def record(kept, slot, block, coef):
        texts_kept = lax.dynamic_update_slice_in_dim(kept[0], block, slot * rows, 0)
        coefs_kept = lax.dynamic_update_slice_in_dim(kept[1], coef, slot * rows, 1)
        return (texts_kept, coefs_kept)

    kept_start = (
        jnp.zeros((loops * rows, width), jnp.bfloat16),
        jnp.zeros((group_rows, loops * rows), jnp.bfloat16),
    )
    stats_start = (jnp.zeros((), jnp.float32), jnp.zeros((), jnp.float32))

    def visit_one(slot, block, sums, kept, stats):
        coef, contrib, loss, count = block_terms(block, ids_of((own_place - slot) % loops, 0, rows))
        return (
            sums + contrib,
            record(kept, slot, block, coef),
            (stats[0] + loss, stats[1] + count),
        )

    def turn_one(slot, carry):
        block, sums, kept, stats = carry
        sums, kept, stats = visit_one(slot, block, sums, kept, stats)
        block = shifted(block, "blk", 1)
        sums = shifted(sums, "blk", 1)
        return (block, sums, kept, stats)

    block, sums, kept, stats = lax.fori_loop(
        0,
        loops - 1,
        turn_one,
        (text_bf, jnp.zeros((rows, width), jnp.float32), kept_start, stats_start),
    )
    sums, kept, stats = visit_one(loops - 1, block, sums, kept, stats)
    text_sums = shifted(sums, "blk", 1)
    texts_kept, coefs_kept = kept
    image_sums = lax.psum_scatter(
        jnp.dot(coefs_kept, texts_kept, preferred_element_type=jnp.float32),
        "grp",
        scatter_dimension=0,
        tiled=True,
    )
    loss_sum, pair_count = lax.psum((stats[0], stats[1]), ("grp", "blk"))
    image_grads = image_back(TEMP * image_sums)[0]
    text_grads = text_back(TEMP * text_sums)[0]
    return (image_grads, text_grads, loss_sum / pair_count)


def solution(mesh):
    return jax.shard_map(
        on_device,
        mesh=mesh,
        in_specs=(P(("blk", "grp"), None), P(("blk", "grp"), None), P()),
        out_specs=(P(("blk", "grp"), None), P(("blk", "grp"), None), P()),
        check_vma=False,
    )
```

profile of v0, /device:TPU:0, one launch (start us, length us, event | category | flops | bytes accessed | tf_op | source)
XLA Modules:
  0.0 194.9 jit_solution(17755911329475531432)
XLA Ops:
  7.2 1.0 fusion.16
  8.2 1.0 fusion.17
  9.2 1.0 fusion.19
  10.3 1.0 fusion.20
  11.2 6.0 %all_gather.3 = bf16[64,1152]{1,0:T(8,128)(2,1)S(1)} all-gather(bf16[32,1152]{1,0:T(8,128)(2,1)S(1)} %fusion.20), channel_id=1, replica_groups=mesh['grp'=2,'blk'=16] {'grp'}, dimensions={0}, use_global_device_ids=true | all-gather | bytes 221184 | tf_op jit(solution)/shard_map/all_gather | solution.py:42
  17.2 0.9 fusion.22
  18.3 121.0 %while.26 = (s32[]{:T(128)}, bf16[32,1152]{1,0:T(8,128)(2,1)S(1)}, f32[32,1152]{1,0:T(8,128)S(1)}, bf16[512,1152]{1,0:T(8,128)(2,1)S(1)}, bf16[64,512]{0,1:T(8,1...) while((s32[]{:T(128)}, bf16[32,1152]{1,0:T(8,128)(2,1)S(1)}, ...), condition=%wide.region_5.6_spmd.clone, body=%wide.region_2.5_spmd.clone.sunk | while | flops 9741141 | bytes 1907960 | solution.py:105
  18.8 0.2 convolution_add_fusion.3
  19.0 2.1 %collective-permute-start.1 = (f32[32,1152]{1,0:T(8,128)S(1)}, f32[32,1152]{1,0:T(8,128)S(1)}, u32[]{:S(2)}, u32[]{:S(2)}) collective-permute-start(f32[32,1152]{1,0:T(8,128)S(1)} %convolution_add_fusion.3), channel_id=1, source_target_pairs={{0,1},{1,2},{2,3},{3,4},{4,5},{5,6},{6,7},{7,8},{8,9},{9,10},{10,1... | collective-permute-start | bytes 442376 | tf_op jit(solution)/shard_map/while/body/eval_jaxpr/ppermute | solution.py:17
  21.2 0.7 convert_reduce_fusion.3
  23.2 1.7 collective-permute-done
  24.8 1.6 collective-permute-done.1
  27.2 0.7 convert_reduce_fusion.3
  29.2 3.7 %collective-permute-done = bf16[32,1152]{1,0:T(8,128)(2,1)S(1)} collective-permute-done((bf16[32,1152]{1,0:T(8,128)(2,1)S(1)}, bf16[32,1152]{1,0:T(8,128)(2,1)S(1)}, u32[]{:S(2)}, u32[]{:S(2)}) %collective-permute-start) | collective-permute-done | bytes 73760 | tf_op jit(solution)/shard_map/while/body/eval_jaxpr/ppermute | solution.py:17
  32.9 1.6 collective-permute-done.1
  35.2 0.7 convert_reduce_fusion.3
  37.2 3.7 %collective-permute-done = bf16[32,1152]{1,0:T(8,128)(2,1)S(1)} collective-permute-done((bf16[32,1152]{1,0:T(8,128)(2,1)S(1)}, bf16[32,1152]{1,0:T(8,128)(2,1)S(1)}, u32[]{:S(2)}, u32[]{:S(2)}) %collective-permute-start) | collective-permute-done | bytes 73760 | tf_op jit(solution)/shard_map/while/body/eval_jaxpr/ppermute | solution.py:17
  40.9 1.6 collective-permute-done.1
  43.0 0.2 convolution_add_fusion.3
  43.3 0.7 convert_reduce_fusion.3
  45.3 3.7 %collective-permute-done = bf16[32,1152]{1,0:T(8,128)(2,1)S(1)} collective-permute-done((bf16[32,1152]{1,0:T(8,128)(2,1)S(1)}, bf16[32,1152]{1,0:T(8,128)(2,1)S(1)}, u32[]{:S(2)}, u32[]{:S(2)}) %collective-permute-start) | collective-permute-done | bytes 73760 | tf_op jit(solution)/shard_map/while/body/eval_jaxpr/ppermute | solution.py:17
  49.0 1.6 collective-permute-done.1
  51.3 0.7 convert_reduce_fusion.3
  53.3 3.7 %collective-permute-done = bf16[32,1152]{1,0:T(8,128)(2,1)S(1)} collective-permute-done((bf16[32,1152]{1,0:T(8,128)(2,1)S(1)}, bf16[32,1152]{1,0:T(8,128)(2,1)S(1)}, u32[]{:S(2)}, u32[]{:S(2)}) %collective-permute-start) | collective-permute-done | bytes 73760 | tf_op jit(solution)/shard_map/while/body/eval_jaxpr/ppermute | solution.py:17
  57.1 1.6 collective-permute-done.1
  59.4 0.7 convert_reduce_fusion.3
  61.4 3.7 %collective-permute-done = bf16[32,1152]{1,0:T(8,128)(2,1)S(1)} collective-permute-done((bf16[32,1152]{1,0:T(8,128)(2,1)S(1)}, bf16[32,1152]{1,0:T(8,128)(2,1)S(1)}, u32[]{:S(2)}, u32[]{:S(2)}) %collective-permute-start) | collective-permute-done | bytes 73760 | tf_op jit(solution)/shard_map/while/body/eval_jaxpr/ppermute | solution.py:17
  65.1 1.6 collective-permute-done.1
  67.5 0.7 convert_reduce_fusion.3
  69.5 3.7 %collective-permute-done = bf16[32,1152]{1,0:T(8,128)(2,1)S(1)} collective-permute-done((bf16[32,1152]{1,0:T(8,128)(2,1)S(1)}, bf16[32,1152]{1,0:T(8,128)(2,1)S(1)}, u32[]{:S(2)}, u32[]{:S(2)}) %collective-permute-start) | collective-permute-done | bytes 73760 | tf_op jit(solution)/shard_map/while/body/eval_jaxpr/ppermute | solution.py:17
  73.2 1.6 collective-permute-done.1
  75.5 0.7 convert_reduce_fusion.3
  77.5 3.7 %collective-permute-done = bf16[32,1152]{1,0:T(8,128)(2,1)S(1)} collective-permute-done((bf16[32,1152]{1,0:T(8,128)(2,1)S(1)}, bf16[32,1152]{1,0:T(8,128)(2,1)S(1)}, u32[]{:S(2)}, u32[]{:S(2)}) %collective-permute-start) | collective-permute-done | bytes 73760 | tf_op jit(solution)/shard_map/while/body/eval_jaxpr/ppermute | solution.py:17
  81.2 1.6 collective-permute-done.1
  83.6 0.7 convert_reduce_fusion.3
  85.6 3.7 %collective-permute-done = bf16[32,1152]{1,0:T(8,128)(2,1)S(1)} collective-permute-done((bf16[32,1152]{1,0:T(8,128)(2,1)S(1)}, bf16[32,1152]{1,0:T(8,128)(2,1)S(1)}, u32[]{:S(2)}, u32[]{:S(2)}) %collective-permute-start) | collective-permute-done | bytes 73760 | tf_op jit(solution)/shard_map/while/body/eval_jaxpr/ppermute | solution.py:17
  89.3 1.6 collective-permute-done.1
  91.7 0.7 convert_reduce_fusion.3
  93.7 3.7 %collective-permute-done = bf16[32,1152]{1,0:T(8,128)(2,1)S(1)} collective-permute-done((bf16[32,1152]{1,0:T(8,128)(2,1)S(1)}, bf16[32,1152]{1,0:T(8,128)(2,1)S(1)}, u32[]{:S(2)}, u32[]{:S(2)}) %collective-permute-start) | collective-permute-done | bytes 73760 | tf_op jit(solution)/shard_map/while/body/eval_jaxpr/ppermute | solution.py:17
  97.4 1.6 collective-permute-done.1
  99.4 0.2 convolution_add_fusion.3
  99.7 0.7 convert_reduce_fusion.3
  101.7 3.7 %collective-permute-done = bf16[32,1152]{1,0:T(8,128)(2,1)S(1)} collective-permute-done((bf16[32,1152]{1,0:T(8,128)(2,1)S(1)}, bf16[32,1152]{1,0:T(8,128)(2,1)S(1)}, u32[]{:S(2)}, u32[]{:S(2)}) %collective-permute-start) | collective-permute-done | bytes 73760 | tf_op jit(solution)/shard_map/while/body/eval_jaxpr/ppermute | solution.py:17
  105.4 1.6 collective-permute-done.1
  107.8 0.7 convert_reduce_fusion.3
  109.8 3.7 %collective-permute-done = bf16[32,1152]{1,0:T(8,128)(2,1)S(1)} collective-permute-done((bf16[32,1152]{1,0:T(8,128)(2,1)S(1)}, bf16[32,1152]{1,0:T(8,128)(2,1)S(1)}, u32[]{:S(2)}, u32[]{:S(2)}) %collective-permute-start) | collective-permute-done | bytes 73760 | tf_op jit(solution)/shard_map/while/body/eval_jaxpr/ppermute | solution.py:17
  113.5 1.6 collective-permute-done.1
  115.8 0.7 convert_reduce_fusion.3
  117.8 3.7 %collective-permute-done = bf16[32,1152]{1,0:T(8,128)(2,1)S(1)} collective-permute-done((bf16[32,1152]{1,0:T(8,128)(2,1)S(1)}, bf16[32,1152]{1,0:T(8,128)(2,1)S(1)}, u32[]{:S(2)}, u32[]{:S(2)}) %collective-permute-start) | collective-permute-done | bytes 73760 | tf_op jit(solution)/shard_map/while/body/eval_jaxpr/ppermute | solution.py:17
  121.6 1.6 collective-permute-done.1
  123.9 0.7 convert_reduce_fusion.3
  125.9 3.7 %collective-permute-done = bf16[32,1152]{1,0:T(8,128)(2,1)S(1)} collective-permute-done((bf16[32,1152]{1,0:T(8,128)(2,1)S(1)}, bf16[32,1152]{1,0:T(8,128)(2,1)S(1)}, u32[]{:S(2)}, u32[]{:S(2)}) %collective-permute-start) | collective-permute-done | bytes 73760 | tf_op jit(solution)/shard_map/while/body/eval_jaxpr/ppermute | solution.py:17
  129.6 1.6 collective-permute-done.1
  131.5 0.2 constant_dynamic-update-slice_fusion.6
  132.0 0.7 convert_reduce_fusion.3
  134.0 3.7 %collective-permute-done = bf16[32,1152]{1,0:T(8,128)(2,1)S(1)} collective-permute-done((bf16[32,1152]{1,0:T(8,128)(2,1)S(1)}, bf16[32,1152]{1,0:T(8,128)(2,1)S(1)}, u32[]{:S(2)}, u32[]{:S(2)}) %collective-permute-start) | collective-permute-done | bytes 73760 | tf_op jit(solution)/shard_map/while/body/eval_jaxpr/ppermute | solution.py:17
  137.7 1.6 collective-permute-done.1
  139.4 0.2 constant_dynamic-update-slice_fusion.3
  140.0 0.8 convert_reduce_fusion.1
  142.1 1.0 fusion.34
  143.2 38.8 %all-reduce = (f32[]{:T(128)}, f32[]{:T(128)}) all-reduce(f32[]{:T(128)S(6)} %add.251, f32[]{:T(128)S(6)} %add.252), channel_id=1, replica_groups=mesh['grp'=2,'blk'=16] {'grp','blk'}, use_global_device_ids=true, to_apply=%region_10.11 | all-reduce | flops 2 | bytes 16 | tf_op jit(solution)/shard_map/psum | solution.py:120
  183.5 0.8 add_add_fusion
  184.2 1.0 fusion.21
  185.3 1.7 add_add_fusion.1
  (152 shorter events, 10.3 us)
Async XLA Ops:
  7.2 177.1 %reduce-scatter.2.cloned.1.call-start = ((), (), s32[]{:S(2)}) async-start(), calls=%async_computation.1 | async-start | bytes 442368 | tf_op jit(solution)/shard_map/reduce_scatter | solution.py:114
  18.3 6.5 %collective-permute-start = (bf16[32,1152]{1,0:T(8,128)(2,1)S(1)}, bf16[32,1152]{1,0:T(8,128)(2,1)S(1)}, u32[]{:S(2)}, u32[]{:S(2)}) collective-permute-start(bf16[32,1152]{1,0:T(8,128)(2,1)S(1)} %copy.16), channel_id=1, source_target_pairs={{0,1},{1,2},{2,3},{3,4},{4,5},{5,6},{6,7},{7,8},{8,9},{9,10},{10,1... | collective-permute-start | bytes 221192 | tf_op jit(solution)/shard_map/while/body/eval_jaxpr/ppermute | solution.py:17
  19.0 7.4 %collective-permute-start.1 = (f32[32,1152]{1,0:T(8,128)S(1)}, f32[32,1152]{1,0:T(8,128)S(1)}, u32[]{:S(2)}, u32[]{:S(2)}) collective-permute-start(f32[32,1152]{1,0:T(8,128)S(1)} %convolution_add_fusion.3), channel_id=1, source_target_pairs={{0,1},{1,2},{2,3},{3,4},{4,5},{5,6},{6,7},{7,8},{8,9},{9,10},{10,1... | collective-permute-start | bytes 442376 | tf_op jit(solution)/shard_map/while/body/eval_jaxpr/ppermute | solution.py:17
  26.4 6.5 %collective-permute-start = (bf16[32,1152]{1,0:T(8,128)(2,1)S(1)}, bf16[32,1152]{1,0:T(8,128)(2,1)S(1)}, u32[]{:S(2)}, u32[]{:S(2)}) collective-permute-start(bf16[32,1152]{1,0:T(8,128)(2,1)S(1)} %copy.16), channel_id=1, source_target_pairs={{0,1},{1,2},{2,3},{3,4},{4,5},{5,6},{6,7},{7,8},{8,9},{9,10},{10,1... | collective-permute-start | bytes 221192 | tf_op jit(solution)/shard_map/while/body/eval_jaxpr/ppermute | solution.py:17
  27.1 7.4 %collective-permute-start.1 = (f32[32,1152]{1,0:T(8,128)S(1)}, f32[32,1152]{1,0:T(8,128)S(1)}, u32[]{:S(2)}, u32[]{:S(2)}) collective-permute-start(f32[32,1152]{1,0:T(8,128)S(1)} %convolution_add_fusion.3), channel_id=1, source_target_pairs={{0,1},{1,2},{2,3},{3,4},{4,5},{5,6},{6,7},{7,8},{8,9},{9,10},{10,1... | collective-permute-start | bytes 442376 | tf_op jit(solution)/shard_map/while/body/eval_jaxpr/ppermute | solution.py:17
  34.5 6.5 %collective-permute-start = (bf16[32,1152]{1,0:T(8,128)(2,1)S(1)}, bf16[32,1152]{1,0:T(8,128)(2,1)S(1)}, u32[]{:S(2)}, u32[]{:S(2)}) collective-permute-start(bf16[32,1152]{1,0:T(8,128)(2,1)S(1)} %copy.16), channel_id=1, source_target_pairs={{0,1},{1,2},{2,3},{3,4},{4,5},{5,6},{6,7},{7,8},{8,9},{9,10},{10,1... | collective-permute-start | bytes 221192 | tf_op jit(solution)/shard_map/while/body/eval_jaxpr/ppermute | solution.py:17
  35.1 7.4 %collective-permute-start.1 = (f32[32,1152]{1,0:T(8,128)S(1)}, f32[32,1152]{1,0:T(8,128)S(1)}, u32[]{:S(2)}, u32[]{:S(2)}) collective-permute-start(f32[32,1152]{1,0:T(8,128)S(1)} %convolution_add_fusion.3), channel_id=1, source_target_pairs={{0,1},{1,2},{2,3},{3,4},{4,5},{5,6},{6,7},{7,8},{8,9},{9,10},{10,1... | collective-permute-start | bytes 442376 | tf_op jit(solution)/shard_map/while/body/eval_jaxpr/ppermute | solution.py:17
  42.5 6.5 %collective-permute-start = (bf16[32,1152]{1,0:T(8,128)(2,1)S(1)}, bf16[32,1152]{1,0:T(8,128)(2,1)S(1)}, u32[]{:S(2)}, u32[]{:S(2)}) collective-permute-start(bf16[32,1152]{1,0:T(8,128)(2,1)S(1)} %copy.16), channel_id=1, source_target_pairs={{0,1},{1,2},{2,3},{3,4},{4,5},{5,6},{6,7},{7,8},{8,9},{9,10},{10,1... | collective-permute-start | bytes 221192 | tf_op jit(solution)/shard_map/while/body/eval_jaxpr/ppermute | solution.py:17
  43.2 7.4 %collective-permute-start.1 = (f32[32,1152]{1,0:T(8,128)S(1)}, f32[32,1152]{1,0:T(8,128)S(1)}, u32[]{:S(2)}, u32[]{:S(2)}) collective-permute-start(f32[32,1152]{1,0:T(8,128)S(1)} %convolution_add_fusion.3), channel_id=1, source_target_pairs={{0,1},{1,2},{2,3},{3,4},{4,5},{5,6},{6,7},{7,8},{8,9},{9,10},{10,1... | collective-permute-start | bytes 442376 | tf_op jit(solution)/shard_map/while/body/eval_jaxpr/ppermute | solution.py:17
  50.6 6.5 %collective-permute-start = (bf16[32,1152]{1,0:T(8,128)(2,1)S(1)}, bf16[32,1152]{1,0:T(8,128)(2,1)S(1)}, u32[]{:S(2)}, u32[]{:S(2)}) collective-permute-start(bf16[32,1152]{1,0:T(8,128)(2,1)S(1)} %copy.16), channel_id=1, source_target_pairs={{0,1},{1,2},{2,3},{3,4},{4,5},{5,6},{6,7},{7,8},{8,9},{9,10},{10,1... | collective-permute-start | bytes 221192 | tf_op jit(solution)/shard_map/while/body/eval_jaxpr/ppermute | solution.py:17
  51.3 7.4 %collective-permute-start.1 = (f32[32,1152]{1,0:T(8,128)S(1)}, f32[32,1152]{1,0:T(8,128)S(1)}, u32[]{:S(2)}, u32[]{:S(2)}) collective-permute-start(f32[32,1152]{1,0:T(8,128)S(1)} %convolution_add_fusion.3), channel_id=1, source_target_pairs={{0,1},{1,2},{2,3},{3,4},{4,5},{5,6},{6,7},{7,8},{8,9},{9,10},{10,1... | collective-permute-start | bytes 442376 | tf_op jit(solution)/shard_map/while/body/eval_jaxpr/ppermute | solution.py:17
  58.6 6.5 %collective-permute-start = (bf16[32,1152]{1,0:T(8,128)(2,1)S(1)}, bf16[32,1152]{1,0:T(8,128)(2,1)S(1)}, u32[]{:S(2)}, u32[]{:S(2)}) collective-permute-start(bf16[32,1152]{1,0:T(8,128)(2,1)S(1)} %copy.16), channel_id=1, source_target_pairs={{0,1},{1,2},{2,3},{3,4},{4,5},{5,6},{6,7},{7,8},{8,9},{9,10},{10,1... | collective-permute-start | bytes 221192 | tf_op jit(solution)/shard_map/while/body/eval_jaxpr/ppermute | solution.py:17
  59.3 7.4 %collective-permute-start.1 = (f32[32,1152]{1,0:T(8,128)S(1)}, f32[32,1152]{1,0:T(8,128)S(1)}, u32[]{:S(2)}, u32[]{:S(2)}) collective-permute-start(f32[32,1152]{1,0:T(8,128)S(1)} %convolution_add_fusion.3), channel_id=1, source_target_pairs={{0,1},{1,2},{2,3},{3,4},{4,5},{5,6},{6,7},{7,8},{8,9},{9,10},{10,1... | collective-permute-start | bytes 442376 | tf_op jit(solution)/shard_map/while/body/eval_jaxpr/ppermute | solution.py:17
  66.7 6.5 %collective-permute-start = (bf16[32,1152]{1,0:T(8,128)(2,1)S(1)}, bf16[32,1152]{1,0:T(8,128)(2,1)S(1)}, u32[]{:S(2)}, u32[]{:S(2)}) collective-permute-start(bf16[32,1152]{1,0:T(8,128)(2,1)S(1)} %copy.16), channel_id=1, source_target_pairs={{0,1},{1,2},{2,3},{3,4},{4,5},{5,6},{6,7},{7,8},{8,9},{9,10},{10,1... | collective-permute-start | bytes 221192 | tf_op jit(solution)/shard_map/while/body/eval_jaxpr/ppermute | solution.py:17
  67.4 7.4 %collective-permute-start.1 = (f32[32,1152]{1,0:T(8,128)S(1)}, f32[32,1152]{1,0:T(8,128)S(1)}, u32[]{:S(2)}, u32[]{:S(2)}) collective-permute-start(f32[32,1152]{1,0:T(8,128)S(1)} %convolution_add_fusion.3), channel_id=1, source_target_pairs={{0,1},{1,2},{2,3},{3,4},{4,5},{5,6},{6,7},{7,8},{8,9},{9,10},{10,1... | collective-permute-start | bytes 442376 | tf_op jit(solution)/shard_map/while/body/eval_jaxpr/ppermute | solution.py:17
  74.8 6.5 %collective-permute-start = (bf16[32,1152]{1,0:T(8,128)(2,1)S(1)}, bf16[32,1152]{1,0:T(8,128)(2,1)S(1)}, u32[]{:S(2)}, u32[]{:S(2)}) collective-permute-start(bf16[32,1152]{1,0:T(8,128)(2,1)S(1)} %copy.16), channel_id=1, source_target_pairs={{0,1},{1,2},{2,3},{3,4},{4,5},{5,6},{6,7},{7,8},{8,9},{9,10},{10,1... | collective-permute-start | bytes 221192 | tf_op jit(solution)/shard_map/while/body/eval_jaxpr/ppermute | solution.py:17
  75.4 7.4 %collective-permute-start.1 = (f32[32,1152]{1,0:T(8,128)S(1)}, f32[32,1152]{1,0:T(8,128)S(1)}, u32[]{:S(2)}, u32[]{:S(2)}) collective-permute-start(f32[32,1152]{1,0:T(8,128)S(1)} %convolution_add_fusion.3), channel_id=1, source_target_pairs={{0,1},{1,2},{2,3},{3,4},{4,5},{5,6},{6,7},{7,8},{8,9},{9,10},{10,1... | collective-permute-start | bytes 442376 | tf_op jit(solution)/shard_map/while/body/eval_jaxpr/ppermute | solution.py:17
  82.8 6.5 %collective-permute-start = (bf16[32,1152]{1,0:T(8,128)(2,1)S(1)}, bf16[32,1152]{1,0:T(8,128)(2,1)S(1)}, u32[]{:S(2)}, u32[]{:S(2)}) collective-permute-start(bf16[32,1152]{1,0:T(8,128)(2,1)S(1)} %copy.16), channel_id=1, source_target_pairs={{0,1},{1,2},{2,3},{3,4},{4,5},{5,6},{6,7},{7,8},{8,9},{9,10},{10,1... | collective-permute-start | bytes 221192 | tf_op jit(solution)/shard_map/while/body/eval_jaxpr/ppermute | solution.py:17
  83.5 7.4 %collective-permute-start.1 = (f32[32,1152]{1,0:T(8,128)S(1)}, f32[32,1152]{1,0:T(8,128)S(1)}, u32[]{:S(2)}, u32[]{:S(2)}) collective-permute-start(f32[32,1152]{1,0:T(8,128)S(1)} %convolution_add_fusion.3), channel_id=1, source_target_pairs={{0,1},{1,2},{2,3},{3,4},{4,5},{5,6},{6,7},{7,8},{8,9},{9,10},{10,1... | collective-permute-start | bytes 442376 | tf_op jit(solution)/shard_map/while/body/eval_jaxpr/ppermute | solution.py:17
  90.9 6.5 %collective-permute-start = (bf16[32,1152]{1,0:T(8,128)(2,1)S(1)}, bf16[32,1152]{1,0:T(8,128)(2,1)S(1)}, u32[]{:S(2)}, u32[]{:S(2)}) collective-permute-start(bf16[32,1152]{1,0:T(8,128)(2,1)S(1)} %copy.16), channel_id=1, source_target_pairs={{0,1},{1,2},{2,3},{3,4},{4,5},{5,6},{6,7},{7,8},{8,9},{9,10},{10,1... | collective-permute-start | bytes 221192 | tf_op jit(solution)/shard_map/while/body/eval_jaxpr/ppermute | solution.py:17
  91.6 7.4 %collective-permute-start.1 = (f32[32,1152]{1,0:T(8,128)S(1)}, f32[32,1152]{1,0:T(8,128)S(1)}, u32[]{:S(2)}, u32[]{:S(2)}) collective-permute-start(f32[32,1152]{1,0:T(8,128)S(1)} %convolution_add_fusion.3), channel_id=1, source_target_pairs={{0,1},{1,2},{2,3},{3,4},{4,5},{5,6},{6,7},{7,8},{8,9},{9,10},{10,1... | collective-permute-start | bytes 442376 | tf_op jit(solution)/shard_map/while/body/eval_jaxpr/ppermute | solution.py:17
  99.0 6.5 %collective-permute-start = (bf16[32,1152]{1,0:T(8,128)(2,1)S(1)}, bf16[32,1152]{1,0:T(8,128)(2,1)S(1)}, u32[]{:S(2)}, u32[]{:S(2)}) collective-permute-start(bf16[32,1152]{1,0:T(8,128)(2,1)S(1)} %copy.16), channel_id=1, source_target_pairs={{0,1},{1,2},{2,3},{3,4},{4,5},{5,6},{6,7},{7,8},{8,9},{9,10},{10,1... | collective-permute-start | bytes 221192 | tf_op jit(solution)/shard_map/while/body/eval_jaxpr/ppermute | solution.py:17
  99.6 7.4 %collective-permute-start.1 = (f32[32,1152]{1,0:T(8,128)S(1)}, f32[32,1152]{1,0:T(8,128)S(1)}, u32[]{:S(2)}, u32[]{:S(2)}) collective-permute-start(f32[32,1152]{1,0:T(8,128)S(1)} %convolution_add_fusion.3), channel_id=1, source_target_pairs={{0,1},{1,2},{2,3},{3,4},{4,5},{5,6},{6,7},{7,8},{8,9},{9,10},{10,1... | collective-permute-start | bytes 442376 | tf_op jit(solution)/shard_map/while/body/eval_jaxpr/ppermute | solution.py:17
  107.0 6.5 %collective-permute-start = (bf16[32,1152]{1,0:T(8,128)(2,1)S(1)}, bf16[32,1152]{1,0:T(8,128)(2,1)S(1)}, u32[]{:S(2)}, u32[]{:S(2)}) collective-permute-start(bf16[32,1152]{1,0:T(8,128)(2,1)S(1)} %copy.16), channel_id=1, source_target_pairs={{0,1},{1,2},{2,3},{3,4},{4,5},{5,6},{6,7},{7,8},{8,9},{9,10},{10,1... | collective-permute-start | bytes 221192 | tf_op jit(solution)/shard_map/while/body/eval_jaxpr/ppermute | solution.py:17
  107.7 7.4 %collective-permute-start.1 = (f32[32,1152]{1,0:T(8,128)S(1)}, f32[32,1152]{1,0:T(8,128)S(1)}, u32[]{:S(2)}, u32[]{:S(2)}) collective-permute-start(f32[32,1152]{1,0:T(8,128)S(1)} %convolution_add_fusion.3), channel_id=1, source_target_pairs={{0,1},{1,2},{2,3},{3,4},{4,5},{5,6},{6,7},{7,8},{8,9},{9,10},{10,1... | collective-permute-start | bytes 442376 | tf_op jit(solution)/shard_map/while/body/eval_jaxpr/ppermute | solution.py:17
  115.1 6.5 %collective-permute-start = (bf16[32,1152]{1,0:T(8,128)(2,1)S(1)}, bf16[32,1152]{1,0:T(8,128)(2,1)S(1)}, u32[]{:S(2)}, u32[]{:S(2)}) collective-permute-start(bf16[32,1152]{1,0:T(8,128)(2,1)S(1)} %copy.16), channel_id=1, source_target_pairs={{0,1},{1,2},{2,3},{3,4},{4,5},{5,6},{6,7},{7,8},{8,9},{9,10},{10,1... | collective-permute-start | bytes 221192 | tf_op jit(solution)/shard_map/while/body/eval_jaxpr/ppermute | solution.py:17
  115.8 7.4 %collective-permute-start.1 = (f32[32,1152]{1,0:T(8,128)S(1)}, f32[32,1152]{1,0:T(8,128)S(1)}, u32[]{:S(2)}, u32[]{:S(2)}) collective-permute-start(f32[32,1152]{1,0:T(8,128)S(1)} %convolution_add_fusion.3), channel_id=1, source_target_pairs={{0,1},{1,2},{2,3},{3,4},{4,5},{5,6},{6,7},{7,8},{8,9},{9,10},{10,1... | collective-permute-start | bytes 442376 | tf_op jit(solution)/shard_map/while/body/eval_jaxpr/ppermute | solution.py:17
  123.1 6.5 %collective-permute-start = (bf16[32,1152]{1,0:T(8,128)(2,1)S(1)}, bf16[32,1152]{1,0:T(8,128)(2,1)S(1)}, u32[]{:S(2)}, u32[]{:S(2)}) collective-permute-start(bf16[32,1152]{1,0:T(8,128)(2,1)S(1)} %copy.16), channel_id=1, source_target_pairs={{0,1},{1,2},{2,3},{3,4},{4,5},{5,6},{6,7},{7,8},{8,9},{9,10},{10,1... | collective-permute-start | bytes 221192 | tf_op jit(solution)/shard_map/while/body/eval_jaxpr/ppermute | solution.py:17
  123.8 7.4 %collective-permute-start.1 = (f32[32,1152]{1,0:T(8,128)S(1)}, f32[32,1152]{1,0:T(8,128)S(1)}, u32[]{:S(2)}, u32[]{:S(2)}) collective-permute-start(f32[32,1152]{1,0:T(8,128)S(1)} %convolution_add_fusion.3), channel_id=1, source_target_pairs={{0,1},{1,2},{2,3},{3,4},{4,5},{5,6},{6,7},{7,8},{8,9},{9,10},{10,1... | collective-permute-start | bytes 442376 | tf_op jit(solution)/shard_map/while/body/eval_jaxpr/ppermute | solution.py:17
  131.2 6.5 %collective-permute-start = (bf16[32,1152]{1,0:T(8,128)(2,1)S(1)}, bf16[32,1152]{1,0:T(8,128)(2,1)S(1)}, u32[]{:S(2)}, u32[]{:S(2)}) collective-permute-start(bf16[32,1152]{1,0:T(8,128)(2,1)S(1)} %copy.16), channel_id=1, source_target_pairs={{0,1},{1,2},{2,3},{3,4},{4,5},{5,6},{6,7},{7,8},{8,9},{9,10},{10,1... | collective-permute-start | bytes 221192 | tf_op jit(solution)/shard_map/while/body/eval_jaxpr/ppermute | solution.py:17
  131.9 7.4 %collective-permute-start.1 = (f32[32,1152]{1,0:T(8,128)S(1)}, f32[32,1152]{1,0:T(8,128)S(1)}, u32[]{:S(2)}, u32[]{:S(2)}) collective-permute-start(f32[32,1152]{1,0:T(8,128)S(1)} %convolution_add_fusion.3), channel_id=1, source_target_pairs={{0,1},{1,2},{2,3},{3,4},{4,5},{5,6},{6,7},{7,8},{8,9},{9,10},{10,1... | collective-permute-start | bytes 442376 | tf_op jit(solution)/shard_map/while/body/eval_jaxpr/ppermute | solution.py:17
  139.7 43.7 %copy-start = (bf16[32,1152]{1,0:T(8,128)(2,1)S(1)}, bf16[32,1152]{1,0:T(8,128)(2,1)}, u32[]{:S(2)}) copy-start(bf16[32,1152]{1,0:T(8,128)(2,1)} %param.6) | copy-start | bytes 221188
  139.9 43.4 %collective-permute-start.2 = (f32[32,1152]{1,0:T(8,128)S(1)}, f32[32,1152]{1,0:T(8,128)S(1)}, u32[]{:S(2)}, u32[]{:S(2)}) collective-permute-start(f32[32,1152]{1,0:T(8,128)S(1)} %convolution_add_fusion.1), channel_id=1, source_target_pairs={{0,1},{1,2},{2,3},{3,4},{4,5},{5,6},{6,7},{7,8},{8,9},{9,10},{10,1... | collective-permute-start | bytes 442376 | tf_op jit(solution)/shard_map/ppermute | solution.py:17
  142.1 42.1 %copy-start.1 = (bf16[32,1152]{1,0:T(8,128)(2,1)S(1)}, bf16[32,1152]{1,0:T(8,128)(2,1)}, u32[]{:S(2)}) copy-start(bf16[32,1152]{1,0:T(8,128)(2,1)} %param.5) | copy-start | bytes 221188
Sparse Core Ops, SparseCore 0:
  143.3 13.8 reduce-scatter.1
where the time goes:
time: 196 us; the launch traced here: 195 us
  waiting for transfers between devices  77.4 us (39%)
  blocking collectives  44.8 us (23%)
  other arithmetic  19.9 us (10%)
  loops' own time  19.9 us (10%)
  between operations  18 us (9%)
  matrix products  11.3 us (6%)
  starting transfers between devices  3.08 us (2%)
    ppermute x31, waiting for transfers between devices, shifted(): return lax.ppermute(value, axis, pairs)  77.4 us
    psum x1, blocking collectives, on_device(): loss_sum, pair_count = lax.psum((stats[0], stats[1]), ('grp', 'blk'))  38.8 us
    another operation x1, loops' own time, on_device(): lax.fori_loop(0, loops - 1, turn_one, (text_bf, jnp.zeros((rows, width),...  19.9 us
    reduce_sum x16, other arithmetic, block_terms(): count = jnp.sum(valid.astype(jnp.float32))  12 us
    all_gather x1, blocking collectives, on_device(): gathered = lax.all_gather(image_bf, 'grp', axis=0, tiled=True)  5.95 us
  transfers between devices with their start and end apart: 32, of which 30 were waited for; matrix products, arithmetic and copies ran while one was open for 12% of the time, Pallas kernels for 0%

commit v1 on v0

v1 whole, which is shorter than its diff:
```python
import functools

import jax
import jax.numpy as jnp
from jax import lax
from jax.experimental import pallas as pl
from jax.experimental.pallas import tpu as pltpu
from jax.sharding import PartitionSpec as P

TILE = 128
TEMP = 10.0
BIAS = -2.0
EPS = 1e-06
MESH = pl.DeviceIdType.MESH


def split_of(groups, loops, rows):
    best = None
    for inner in range(1, loops + 1):
        if loops % inner or (groups * inner * rows) % TILE:
            continue
        cost = groups * inner + loops // inner
        if best is None or cost <= best[0]:
            best = (cost, inner)
    return best[1]


def inverse_norm(x):
    return lax.rsqrt(jnp.sum(x * x, axis=-1, keepdims=True) + EPS)


def backward(x, g):
    r = inverse_norm(x)
    u = x * r
    return r * (g - u * jnp.sum(u * g, axis=-1, keepdims=True))


def each(count, body):
    if count == 1:
        body(0)
    else:
        lax.fori_loop(0, count, lambda i, c: (body(i), c)[1], 0)


def kernel(groups, loops, inner, mask_s, mask_v, img_ref, txt_ref,
           img_out, txt_out, loss_out,
           imgs, txts, coef, img_part, txt_part, img_in, txt_in, loss_a, loss_b,
           img_send, img_recv, txt_send, txt_recv,
           ip_send, ip_recv, tp_send, tp_recv,
           la_send, la_recv, lb_send, lb_recv):
    rows = img_ref.shape[0]
    across = groups * inner
    along = loops // inner
    g = lax.axis_index("grp")
    b = lax.axis_index("blk")
    o, i = b // inner, b % inner
    m = i * groups + g
    wide, tall = across * rows, along * rows

    def image_peer(d):
        p = lax.rem(m + d, across)
        return p, {"grp": p % groups, "blk": o * inner + p // groups}

    def text_peer(d):
        p = lax.rem(o + d, along)
        return p, {"grp": g, "blk": p * inner + i}

    def block(ref, p):
        return ref.at[pl.ds(pl.multiple_of(p * rows, rows), rows)]

    def copy(src, dst, send, recv, to):
        return pltpu.make_async_remote_copy(
            src_ref=src, dst_ref=dst, send_sem=send, recv_sem=recv,
            device_id=to, device_id_type=MESH)

    def image_copy(d, arriving=False):
        p, to = image_peer(d)
        at = p if arriving else m
        return copy(block(imgs, at), block(imgs, at), img_send.at[d], img_recv.at[at], to)

    def text_copy(d, arriving=False):
        p, to = text_peer(d)
        at = p if arriving else o
        return copy(block(txts, at), block(txts, at), txt_send.at[d], txt_recv.at[at], to)

    def image_sum_copy(d, arriving=False):
        p, to = image_peer(d)
        at = p if arriving else m
        return copy(block(img_part, p), img_in.at[at], ip_send.at[d], ip_recv.at[at], to)

    def text_sum_copy(d, arriving=False):
        p, to = text_peer(d)
        at = p if arriving else o
        return copy(block(txt_part, p), txt_in.at[at], tp_send.at[d], tp_recv.at[at], to)

    def loss_a_copy(d, arriving=False):
        p, to = image_peer(d)
        at = p if arriving else m
        return copy(loss_a.at[m], loss_a.at[at], la_send.at[d], la_recv.at[at], to)

    def loss_b_copy(d, arriving=False):
        p, to = text_peer(d)
        at = p if arriving else o
        return copy(loss_b.at[o], loss_b.at[at], lb_send.at[d], lb_recv.at[at], to)

    barrier = pltpu.get_barrier_semaphore()
    for d in range(1, along):
        pl.semaphore_signal(barrier, inc=1, device_id=text_peer(d)[1], device_id_type=MESH)
    for d in range(1, across):
        pl.semaphore_signal(barrier, inc=1, device_id=image_peer(d)[1], device_id_type=MESH)

    x = txt_ref[...].astype(jnp.float32)
    block(txts, o)[...] = (x * inverse_norm(x)).astype(jnp.bfloat16)
    x = img_ref[...].astype(jnp.float32)
    block(imgs, m)[...] = (x * inverse_norm(x)).astype(jnp.bfloat16)
    pl.semaphore_wait(barrier, along + across - 2)

    for d in range(1, along):
        text_copy(d).start()
    for d in range(1, across):
        image_copy(d).start()
    loss_a[m] = jnp.zeros_like(loss_a[m])
    for d in range(1, across):
        image_copy(d, True).wait_recv()
    for d in range(1, along):
        text_copy(d, True).wait_recv()

    tb, ib = min(tall, 128), min(wide, 256)
    pieces = tb // rows

    def terms(step):
        t, n = step // (wide // ib), step % (wide // ib)
        t_at, n_at = pl.multiple_of(t * tb, tb), pl.multiple_of(n * ib, ib)
        logits = TEMP * lax.dot_general(
            txts[pl.ds(t_at, tb)], imgs[pl.ds(n_at, ib)],
            (((1,), (1,)), ((), ())), preferred_element_type=jnp.float32) + BIAS
        held, ids = [], []
        iota = lax.broadcasted_iota(jnp.int32, (rows, TILE), 0)
        for k in range(pieces):
            start = (((t * pieces + k) * inner + i) * groups + g) * rows
            held.append(jnp.concatenate([
                jnp.full((rows, TILE), mask_s[start // TILE, (o * wide + n_at) // TILE + j], jnp.int32)
                for j in range(ib // TILE)], axis=1))
            ids.append(jnp.concatenate([start + iota] * (ib // TILE), axis=1))
        held, text_ids = jnp.concatenate(held, axis=0), jnp.concatenate(ids, axis=0)
        image_ids = o * wide + n_at + lax.broadcasted_iota(jnp.int32, (tb, ib), 1)
        matched = text_ids == image_ids
        valid = (held == 0) | matched
        z = jnp.where(matched, -logits, logits)
        e = jnp.exp(-jnp.abs(logits))
        loss = jnp.where(valid, jnp.maximum(z, 0.0) + jnp.log1p(e), 0.0)
        sig = jnp.where(logits >= 0, 1.0, e) / (1.0 + e)
        value = jnp.where(valid, sig - matched.astype(jnp.float32), 0.0)
        coef[pl.ds(t_at, tb), pl.ds(n_at, ib)] = value.astype(jnp.bfloat16)
        loss = sum(loss[:, j * TILE:(j + 1) * TILE] for j in range(ib // TILE))
        loss_a[m] += jnp.sum(loss.reshape(tb // 8, 8, TILE), axis=0)

    each((tall // tb) * (wide // ib), terms)
    for d in range(1, across):
        loss_a_copy(d).start()

    def text_sums(t):
        t_at = pl.multiple_of(t * tb, tb)
        txt_part[pl.ds(t_at, tb)] = jnp.dot(
            coef[pl.ds(t_at, tb)], imgs[...], preferred_element_type=jnp.float32)

    each(tall // tb, text_sums)
    for d in range(1, along):
        text_sum_copy(d).start()

    def image_sums(n):
        n_at = pl.multiple_of(n * ib, ib)
        img_part[pl.ds(n_at, ib)] = lax.dot_general(
            coef[:, pl.ds(n_at, ib)], txts[...], (((0,), (0,)), ((), ())),
            preferred_element_type=jnp.float32)

    each(wide // ib, image_sums)
    for d in range(1, across):
        image_sum_copy(d).start()

    for d in range(1, across):
        loss_a_copy(d, True).wait_recv()
    loss_b[o] = jnp.sum(loss_a[...], axis=0)
    for d in range(1, along):
        loss_b_copy(d).start()

    total = block(img_part, m)[...]
    for d in range(1, across):
        image_sum_copy(d, True).wait_recv()
        total += img_in[image_peer(d)[0]]
    img_out[...] = backward(img_ref[...].astype(jnp.float32), TEMP * total)

    for d in range(1, along):
        loss_b_copy(d, True).wait_recv()
    loss = jnp.sum(jnp.sum(loss_b[...], axis=0), keepdims=True)
    open_tiles = jnp.sum((mask_v[...] == 0).astype(jnp.float32), keepdims=True)
    loss_out[...] = loss / (open_tiles * (TILE * TILE) + (loops * groups * rows))

    total = block(txt_part, o)[...]
    for d in range(1, along):
        text_sum_copy(d, True).wait_recv()
        total += txt_in[text_peer(d)[0]]
    txt_out[...] = backward(txt_ref[...].astype(jnp.float32), TEMP * total)

    for d in range(1, across):
        image_copy(d).wait_send()
        image_sum_copy(d).wait_send()
        loss_a_copy(d).wait_send()
    for d in range(1, along):
        text_copy(d).wait_send()
        text_sum_copy(d).wait_send()
        loss_b_copy(d).wait_send()


def solution(mesh):
    groups, loops = mesh.shape["grp"], mesh.shape["blk"]

    def on_device(images, texts, tile_mask):
        rows, width = images.shape
        inner = split_of(groups, loops, rows)
        across, along = groups * inner, loops // inner
        wide, tall = across * rows, along * rows
        dma = pltpu.SemaphoreType.DMA
        vmem = pl.BlockSpec(memory_space=pltpu.VMEM)
        image_grads, text_grads, loss = pl.pallas_call(
            functools.partial(kernel, groups, loops, inner),
            out_shape=(
                jax.ShapeDtypeStruct((rows, width), jnp.float32),
                jax.ShapeDtypeStruct((rows, width), jnp.float32),
                jax.ShapeDtypeStruct((1, 1), jnp.float32),
            ),
            in_specs=[pl.BlockSpec(memory_space=pltpu.SMEM), vmem, vmem, vmem],
            out_specs=(vmem, vmem, vmem),
            scratch_shapes=[
                pltpu.VMEM((wide, width), jnp.bfloat16),
                pltpu.VMEM((tall, width), jnp.bfloat16),
                pltpu.VMEM((tall, wide), jnp.bfloat16),
                pltpu.VMEM((wide, width), jnp.float32),
                pltpu.VMEM((tall, width), jnp.float32),
                pltpu.VMEM((across, rows, width), jnp.float32),
                pltpu.VMEM((along, rows, width), jnp.float32),
                pltpu.VMEM((across, 8, TILE), jnp.float32),
                pltpu.VMEM((along, 8, TILE), jnp.float32),
            ] + [dma((across,)), dma((across,)), dma((along,)), dma((along,))] * 3,
            compiler_params=pltpu.CompilerParams(
                collective_id=0, has_side_effects=True, vmem_limit_bytes=40 * 2**20),
        )(tile_mask, tile_mask, images, texts)
        return image_grads, text_grads, loss[0, 0]

    return jax.shard_map(
        on_device,
        mesh=mesh,
        in_specs=(P(("blk", "grp"), None), P(("blk", "grp"), None), P()),
        out_specs=(P(("blk", "grp"), None), P(("blk", "grp"), None), P()),
        check_vma=False,
    )
```

time: 196 us -> 37.4 us (0.19)
  waiting for transfers between devices: 77.4 us -> 0 us
  blocking collectives: 44.8 us -> 0 us
  Pallas kernels: 0 us -> 31 us
  other arithmetic: 19.9 us -> 0 us
  loops' own time: 19.9 us -> 0 us
  between operations: 18 us -> 2.39 us
  matrix products: 11.3 us -> 0 us
  local copies, waits for them, and re-layouts: 0.57 us -> 3.77 us
  starting transfers between devices: 3.08 us -> 0 us
    ppermute x31 -> x0, waiting for transfers between devices: 77.4 us -> none  [shifted(): return lax.ppermute(value, axis, pairs)]
    psum x1 -> x0, blocking collectives: 38.8 us -> none  [on_device(): loss_sum, pair_count = lax.psum((stats[0], stats[1]), ('grp', 'blk'))]
    pallas_call x0 -> x1, Pallas kernels: none -> 31 us  [on_device(): pl.pallas_call(functools.partial(kernel, groups, loops, inner), out_shape...]
    another operation x1 -> x0, loops' own time: 19.9 us -> none  [on_device(): lax.fori_loop(0, loops - 1, turn_one, (text_bf, jnp.zeros((rows, width),...]
    reduce_sum x20 -> x0, other arithmetic: 15.2 us -> none  [the longest x16 12 us: block_terms(): count = jnp.sum(valid.astype(jnp.float32))]
    dot_general x50 -> x0, matrix products: 11.3 us -> none  [the longest x16 3.45 us: block_terms(): lax.dot_general(coef, gathered, (((0,), (0,)), ((), ())), preferred_eleme...]
    all_gather x1 -> x0, blocking collectives: 5.95 us -> none  [on_device(): gathered = lax.all_gather(image_bf, 'grp', axis=0, tiled=True)]
    unnamed x4 -> x8, local copies, waits for them, and re-layouts: 0.01 us -> 3.77 us
  transfers between devices with their start and end apart: 32 -> 0, of which waited for: 30 -> 0; matrix products, arithmetic and copies ran while one was open for 12% -> 0% of each run, Pallas kernels for 0% -> 0%
where the time goes in v1:
time: 37.4 us; the launch traced here: 37.2 us
  Pallas kernels  31 us (83%)
  local copies, waits for them, and re-layouts  3.77 us (10%)
  between operations  2.39 us (6%)
    pallas_call x1, Pallas kernels, on_device(): pl.pallas_call(functools.partial(kernel, groups, loops, inner), out_shape...  31 us
    unnamed x8, local copies, waits for them, and re-layouts  3.77 us

profile of v1, /device:TPU:0, one launch (start us, length us, event | category | flops | bytes accessed | tf_op | source)
XLA Modules:
  0.0 37.2 jit_solution(15916661595807374110)
XLA Ops:
  0.6 0.0 copy-start
  0.6 0.9 %copy-done = bf16[32,1152]{1,0:T(8,128)(2,1)S(1)} copy-done((bf16[32,1152]{1,0:T(8,128)(2,1)S(1)}, bf16[32,1152]{1,0:T(8,128)(2,1)}, u32[]{:S(2)}) %copy-start) | copy-done | bytes 73752
  1.5 0.0 copy-start.1
  1.5 0.9 %copy-done.1 = bf16[32,1152]{1,0:T(8,128)(2,1)S(1)} copy-done((bf16[32,1152]{1,0:T(8,128)(2,1)S(1)}, bf16[32,1152]{1,0:T(8,128)(2,1)}, u32[]{:S(2)}) %copy-start.1) | copy-done | bytes 73752
  2.4 0.0 copy-start.2
  2.4 0.7 %copy-done.2 = s32[8,8]{1,0:T(8,128)S(1)} copy-done((s32[8,8]{1,0:T(8,128)S(1)}, s32[8,8]{1,0:T(8,128)}, u32[]{:S(2)}) %copy-start.2) | copy-done | bytes 280
  3.1 31.0 %shard_map.58 = (f32[32,1152]{1,0:T(8,128)S(1)}, f32[32,1152]{1,0:T(8,128)S(1)}, f32[1,1]{1,0:T(1,128)}) custom-call(s32[8,8]{1,0:T(8,128)S(1)} %copy-done.2, s32[8,8]{1,0:T(8,128)S(1)} %copy-done.2, bf16[32,1152]{1,0:T(8,128)(2,1)S(1)} %copy-done, bf16[32,1152]{1,0:T(8,128)(2,1)S(1)} %copy-done.1), custom_call_target="tpu_custom_call" | custom-call | tf_op jit(solution)/shard_map/pallas_call | solution.py:225
  34.1 0.7 %copy.9 = f32[32,1152]{1,0:T(8,128)} copy(f32[32,1152]{1,0:T(8,128)S(1)} %get-tuple-element.12) | data formatting | bytes 294912
  34.8 0.7 %copy.10 = f32[32,1152]{1,0:T(8,128)} copy(f32[32,1152]{1,0:T(8,128)S(1)} %get-tuple-element.13) | data formatting | bytes 294912
Async XLA Ops:
  0.6 0.9 %copy-start = (bf16[32,1152]{1,0:T(8,128)(2,1)S(1)}, bf16[32,1152]{1,0:T(8,128)(2,1)}, u32[]{:S(2)}) copy-start(bf16[32,1152]{1,0:T(8,128)(2,1)} %img_ref.1) | copy-start | bytes 221188
  1.5 0.9 %copy-start.1 = (bf16[32,1152]{1,0:T(8,128)(2,1)S(1)}, bf16[32,1152]{1,0:T(8,128)(2,1)}, u32[]{:S(2)}) copy-start(bf16[32,1152]{1,0:T(8,128)(2,1)} %txt_ref.1) | copy-start | bytes 221188
  2.4 0.7 %copy-start.2 = (s32[8,8]{1,0:T(8,128)S(1)}, s32[8,8]{1,0:T(8,128)}, u32[]{:S(2)}) copy-start(s32[8,8]{1,0:T(8,128)} %mask_v.1) | copy-start | bytes 772

commit v2 on v1

v2 whole, which is shorter than its diff:
```python
import functools

import jax
import jax.numpy as jnp
from jax import lax
from jax.experimental import pallas as pl
from jax.experimental.pallas import tpu as pltpu
from jax.sharding import PartitionSpec as P

TILE = 128
TEMP = 10.0
BIAS = -2.0
EPS = 1e-06
LOG_2 = 0.6931471805599453
MESH = pl.DeviceIdType.MESH


def split_of(groups, loops, rows):
    best = None
    for inner in range(1, loops + 1):
        if loops % inner or (groups * inner * rows) % TILE:
            continue
        cost = groups * inner + loops // inner
        if best is None or cost <= best[0]:
            best = (cost, inner)
    return best[1]


def inverse_norm(x):
    return lax.rsqrt(jnp.sum(x * x, axis=-1, keepdims=True) + EPS)


def backward(x, g):
    r = inverse_norm(x)
    u = x * r
    return r * (g - u * jnp.sum(u * g, axis=-1, keepdims=True))


def flipped(place, bits):
    bit = 1
    while bit <= bits:
        if bits & bit:
            place = place + bit - 2 * bit * ((place // bit) % 2)
        bit *= 2
    return place


def step_of(exponent):
    return jnp.exp((exponent - 15.0) * LOG_2)


def pack(value):
    half = value.shape[0] // 2
    most = jnp.max(jnp.abs(value), axis=-1, keepdims=True)
    exponent = jnp.floor(jnp.log(jnp.maximum(most, 1e-30)) * (1.0 / LOG_2)) + 1.0
    fixed = jnp.clip(jnp.round(value * (1.0 / step_of(exponent))), -32767.0, 32767.0)
    fixed = jnp.concatenate(
        [fixed, jnp.broadcast_to(exponent, (value.shape[0], 128))], axis=1).astype(jnp.int32)
    return fixed[:half] * 65536 + (fixed[half:] & 65535)


def unpack(words):
    low = lax.shift_right_arithmetic(lax.shift_left(words, 16), 16)
    fixed = jnp.concatenate([lax.shift_right_arithmetic(words, 16), low], axis=0).astype(jnp.float32)
    width = fixed.shape[1] - 128
    return fixed[:, :width] * step_of(fixed[:, width:width + 1])


def kernel(groups, loops, inner, mask_hbm, img_hbm, txt_hbm,
           img_out, txt_out, loss_out,
           mask_s, mask_v, img_ref, txt_ref,
           imgs, txts, coef, img_part, txt_part, img_go, txt_go, img_in, txt_in, loss_a, loss_b,
           load_sem,
           img_send, img_recv, txt_send, txt_recv,
           ip_send, ip_recv, tp_send, tp_recv,
           la_send, la_recv, lb_send, lb_recv):
    rows = img_ref.shape[0]
    across = groups * inner
    along = loops // inner
    g = lax.axis_index("grp")
    b = lax.axis_index("blk")
    o, i = b // inner, b % inner
    m = i * groups + g
    wide, tall = across * rows, along * rows
    core = groups

    def image_peer(d):
        p = flipped(m, d)
        return p, {"grp": p % groups, "blk": o * inner + p // groups}

    def text_peer(d):
        p = flipped(o, d)
        return p, {"grp": g, "blk": p * inner + i}

    def block(ref, p):
        return ref.at[pl.ds(pl.multiple_of(p * rows, rows), rows)]

    def copy(src, dst, send, recv, to):
        return pltpu.make_async_remote_copy(
            src_ref=src, dst_ref=dst, send_sem=send, recv_sem=recv,
            device_id=to, device_id_type=MESH)

    near = [d for d in range(1, across) if not d & core]

    def image_copy(d):
        return copy(block(imgs, m), block(imgs, m), img_send.at[d], img_recv.at[m], image_peer(d)[1])

    def image_relay(d):
        p = flipped(m, d)
        return copy(block(imgs, p), block(imgs, p), img_send.at[d + core], img_recv.at[p],
                    image_peer(core)[1])

    def image_arrival(d):
        p = flipped(m, d)
        return copy(block(imgs, p), block(imgs, p), img_send.at[d], img_recv.at[p], image_peer(d)[1])

    def text_copy(d, arriving=False):
        p, to = text_peer(d)
        at = p if arriving else o
        return copy(block(txts, at), block(txts, at), txt_send.at[d], txt_recv.at[at], to)

    def image_sum_copy(d, arriving=False):
        p, to = image_peer(d)
        at = p if arriving else m
        return copy(img_go.at[p], img_in.at[at], ip_send.at[d], ip_recv.at[at], to)

    def text_sum_copy(d, arriving=False):
        p, to = text_peer(d)
        at = p if arriving else o
        return copy(txt_go.at[p], txt_in.at[at], tp_send.at[d], tp_recv.at[at], to)

    def loss_a_copy(d, arriving=False):
        p, to = image_peer(d)
        at = p if arriving else m
        return copy(loss_a.at[m], loss_a.at[at], la_send.at[d], la_recv.at[at], to)

    def loss_b_copy(d, arriving=False):
        p, to = text_peer(d)
        at = p if arriving else o
        return copy(loss_b.at[o], loss_b.at[at], lb_send.at[d], lb_recv.at[at], to)

    loads = [pltpu.make_async_copy(src, dst, load_sem.at[k]) for k, (src, dst) in enumerate(
        [(txt_hbm, txt_ref), (img_hbm, img_ref), (mask_hbm, mask_s), (mask_hbm, mask_v)])]
    for load in loads:
        load.start()
    barrier = pltpu.get_barrier_semaphore()
    for d in range(1, along):
        pl.semaphore_signal(barrier, inc=1, device_id=text_peer(d)[1], device_id_type=MESH)
    for d in range(1, across):
        pl.semaphore_signal(barrier, inc=1, device_id=image_peer(d)[1], device_id_type=MESH)

    loads[0].wait()
    x = txt_ref[...].astype(jnp.float32)
    block(txts, o)[...] = (x * inverse_norm(x)).astype(jnp.bfloat16)
    loads[1].wait()
    x = img_ref[...].astype(jnp.float32)
    block(imgs, m)[...] = (x * inverse_norm(x)).astype(jnp.bfloat16)
    pl.semaphore_wait(barrier, along + across - 2)

    for d in range(1, along):
        text_copy(d).start()
    for d in near + [core]:
        image_copy(d).start()
    loads[2].wait()
    loads[3].wait()
    for d in near:
        image_arrival(d).wait_recv()
        image_relay(d).start()
    for d in [core] + [d + core for d in near]:
        image_arrival(d).wait_recv()

    image_ids = o * wide + lax.broadcasted_iota(jnp.int32, (rows, wide), 1)
    iota = lax.broadcasted_iota(jnp.int32, (rows, wide), 0)
    loss = jnp.zeros((rows, TILE), jnp.float32)
    for d in range(along):
        p = flipped(o, d)
        if d:
            text_copy(d, True).wait_recv()
        logits = TEMP * lax.dot_general(
            block(txts, p)[...], imgs[...], (((1,), (1,)), ((), ())),
            preferred_element_type=jnp.float32) + BIAS
        start = ((p * inner + i) * groups + g) * rows
        held = jnp.concatenate([
            jnp.full((rows, TILE), mask_s[start // TILE, (o * wide) // TILE + j], jnp.int32)
            for j in range(wide // TILE)], axis=1)
        matched = start + iota == image_ids
        valid = (held == 0) | matched
        z = jnp.where(matched, -logits, logits)
        e = jnp.exp(-jnp.abs(logits))
        terms = jnp.where(valid, jnp.maximum(z, 0.0) + jnp.log1p(e), 0.0)
        loss += sum(terms[:, j * TILE:(j + 1) * TILE] for j in range(wide // TILE))
        sig = jnp.where(logits >= 0, 1.0, e) / (1.0 + e)
        value = jnp.where(valid, sig - matched.astype(jnp.float32), 0.0).astype(jnp.bfloat16)
        block(coef, p)[...] = value
        sums = jnp.dot(value, imgs[...], preferred_element_type=jnp.float32)
        if d:
            txt_go[p] = pack(sums)
            text_sum_copy(d).start()
        else:
            txt_part[...] = sums
    loss_a[m] = jnp.sum(loss.reshape(rows // 8, 8, TILE), axis=0)
    for d in range(1, across):
        loss_a_copy(d).start()

    img_part[...] = lax.dot_general(
        coef[...], txts[...], (((0,), (0,)), ((), ())), preferred_element_type=jnp.float32)
    for d in reversed(range(1, across)):
        p = flipped(m, d)
        img_go[p] = pack(block(img_part, p)[...])
        image_sum_copy(d).start()

    for d in range(1, across):
        loss_a_copy(d, True).wait_recv()
    loss_b[o] = jnp.sum(loss_a[...], axis=0)
    for d in range(1, along):
        loss_b_copy(d).start()

    total = txt_part[...]
    for d in range(1, along):
        text_sum_copy(d, True).wait_recv()
        total += unpack(txt_in[flipped(o, d)])
    txt_out[...] = backward(txt_ref[...].astype(jnp.float32), TEMP * total)

    for d in range(1, along):
        loss_b_copy(d, True).wait_recv()
    loss = jnp.sum(jnp.sum(loss_b[...], axis=0), keepdims=True)
    open_tiles = jnp.sum((mask_v[...] == 0).astype(jnp.float32), keepdims=True)
    loss_out[...] = loss / (open_tiles * (TILE * TILE) + (loops * groups * rows))

    total = block(img_part, m)[...]
    for d in reversed(range(1, across)):
        image_sum_copy(d, True).wait_recv()
        total += unpack(img_in[flipped(m, d)])
    img_out[...] = backward(img_ref[...].astype(jnp.float32), TEMP * total)

    for d in near:
        image_relay(d).wait_send()
    for d in near + [core]:
        image_copy(d).wait_send()
    for d in range(1, across):
        image_sum_copy(d).wait_send()
        loss_a_copy(d).wait_send()
    for d in range(1, along):
        text_copy(d).wait_send()
        text_sum_copy(d).wait_send()
        loss_b_copy(d).wait_send()


def solution(mesh):
    groups, loops = mesh.shape["grp"], mesh.shape["blk"]

    def on_device(images, texts, tile_mask):
        rows, width = images.shape
        inner = split_of(groups, loops, rows)
        across, along = groups * inner, loops // inner
        wide, tall = across * rows, along * rows
        dma = pltpu.SemaphoreType.DMA
        vmem = pl.BlockSpec(memory_space=pltpu.VMEM)
        image_grads, text_grads, loss = pl.pallas_call(
            functools.partial(kernel, groups, loops, inner),
            out_shape=(
                jax.ShapeDtypeStruct((rows, width), jnp.float32),
                jax.ShapeDtypeStruct((rows, width), jnp.float32),
                jax.ShapeDtypeStruct((1, 1), jnp.float32),
            ),
            in_specs=[pl.BlockSpec(memory_space=pltpu.HBM)] * 3,
            out_specs=(vmem, vmem, vmem),
            scratch_shapes=[
                pltpu.SMEM(tile_mask.shape, jnp.int32),
                pltpu.VMEM(tile_mask.shape, jnp.int32),
                pltpu.VMEM((rows, width), jnp.bfloat16),
                pltpu.VMEM((rows, width), jnp.bfloat16),
                pltpu.VMEM((wide, width), jnp.bfloat16),
                pltpu.VMEM((tall, width), jnp.bfloat16),
                pltpu.VMEM((tall, wide), jnp.bfloat16),
                pltpu.VMEM((wide, width), jnp.float32),
                pltpu.VMEM((rows, width), jnp.float32),
                pltpu.VMEM((across, rows // 2, width + 128), jnp.int32),
                pltpu.VMEM((along, rows // 2, width + 128), jnp.int32),
                pltpu.VMEM((across, rows // 2, width + 128), jnp.int32),
                pltpu.VMEM((along, rows // 2, width + 128), jnp.int32),
                pltpu.VMEM((across, 8, TILE), jnp.float32),
                pltpu.VMEM((along, 8, TILE), jnp.float32),
                dma((4,)),
            ] + [dma((across,)), dma((across,)), dma((along,)), dma((along,))] * 3,
            compiler_params=pltpu.CompilerParams(
                collective_id=0, has_side_effects=True, vmem_limit_bytes=48 * 2**20),
        )(tile_mask, images, texts)
        return image_grads, text_grads, loss[0, 0]

    return jax.shard_map(
        on_device,
        mesh=mesh,
        in_specs=(P(("blk", "grp"), None), P(("blk", "grp"), None), P()),
        out_specs=(P(("blk", "grp"), None), P(("blk", "grp"), None), P()),
        check_vma=False,
    )
```

time: 37.4 us -> 32.2 us (0.86)
  Pallas kernels: 31 us -> 25.7 us
    pallas_call x1, Pallas kernels: 31 us -> 25.7 us  [on_device(): pl.pallas_call(functools.partial(kernel, groups, loops, inner), out_shape...]
where the time goes in v2:
time: 32.2 us; the launch traced here: 31.9 us
  Pallas kernels  25.7 us (80%)
  local copies, waits for them, and re-layouts  3.77 us (12%)
  between operations  2.39 us (7%)
    pallas_call x1, Pallas kernels, on_device(): pl.pallas_call(functools.partial(kernel, groups, loops, inner), out_shape...  25.7 us
    unnamed x8, local copies, waits for them, and re-layouts  3.77 us

profile of v2, /device:TPU:0, one launch (start us, length us, event | category | flops | bytes accessed | tf_op | source)
XLA Modules:
  0.0 31.9 jit_solution(8018616867603232531)
XLA Ops:
  0.6 0.0 copy-start
  0.6 0.9 %copy-done = bf16[32,1152]{1,0:T(8,128)(2,1)S(1)} copy-done((bf16[32,1152]{1,0:T(8,128)(2,1)S(1)}, bf16[32,1152]{1,0:T(8,128)(2,1)}, u32[]{:S(2)}) %copy-start) | copy-done | bytes 73752
  1.5 0.0 copy-start.1
  1.5 0.9 %copy-done.1 = bf16[32,1152]{1,0:T(8,128)(2,1)S(1)} copy-done((bf16[32,1152]{1,0:T(8,128)(2,1)S(1)}, bf16[32,1152]{1,0:T(8,128)(2,1)}, u32[]{:S(2)}) %copy-start.1) | copy-done | bytes 73752
  2.4 0.0 copy-start.2
  2.4 0.7 %copy-done.2 = s32[8,8]{1,0:T(8,128)S(1)} copy-done((s32[8,8]{1,0:T(8,128)S(1)}, s32[8,8]{1,0:T(8,128)}, u32[]{:S(2)}) %copy-start.2) | copy-done | bytes 280
  3.1 25.7 %shard_map.58 = (f32[32,1152]{1,0:T(8,128)S(1)}, f32[32,1152]{1,0:T(8,128)S(1)}, f32[1,1]{1,0:T(1,128)}) custom-call(s32[8,8]{1,0:T(8,128)S(1)} %copy-done.2, bf16[32,1152]{1,0:T(8,128)(2,1)S(1)} %copy-done, bf16[32,1152]{1,0:T(8,128)(2,1)S(1)} %copy-done.1), custom_call_target="tpu_custom_call" | custom-call | tf_op jit(solution)/shard_map/pallas_call | solution.py:259
  28.8 0.7 %copy.9 = f32[32,1152]{1,0:T(8,128)} copy(f32[32,1152]{1,0:T(8,128)S(1)} %get-tuple-element.12) | data formatting | bytes 294912
  29.5 0.7 %copy.10 = f32[32,1152]{1,0:T(8,128)} copy(f32[32,1152]{1,0:T(8,128)S(1)} %get-tuple-element.13) | data formatting | bytes 294912
Async XLA Ops:
  0.6 0.9 %copy-start = (bf16[32,1152]{1,0:T(8,128)(2,1)S(1)}, bf16[32,1152]{1,0:T(8,128)(2,1)}, u32[]{:S(2)}) copy-start(bf16[32,1152]{1,0:T(8,128)(2,1)} %img_hbm.1) | copy-start | bytes 221188
  1.5 0.9 %copy-start.1 = (bf16[32,1152]{1,0:T(8,128)(2,1)S(1)}, bf16[32,1152]{1,0:T(8,128)(2,1)}, u32[]{:S(2)}) copy-start(bf16[32,1152]{1,0:T(8,128)(2,1)} %txt_hbm.1) | copy-start | bytes 221188
  2.4 0.7 %copy-start.2 = (s32[8,8]{1,0:T(8,128)S(1)}, s32[8,8]{1,0:T(8,128)}, u32[]{:S(2)}) copy-start(s32[8,8]{1,0:T(8,128)} %mask_hbm.1) | copy-start | bytes 772

commit v3 on v2

--- a/solution.py
+++ b/solution.py
@@ -69,8 +69,9 @@
 def kernel(groups, loops, inner, mask_hbm, img_hbm, txt_hbm,
            img_out, txt_out, loss_out,
            mask_s, mask_v, img_ref, txt_ref,
-           imgs, txts, coef, img_part, txt_part, img_go, txt_go, img_in, txt_in, loss_a, loss_b,
-           load_sem,
+           imgs, txts, coef, img_part, txt_part, img_go, txt_go, img_in, txt_in, sib_in,
+           img_res, txt_res, loss_a, loss_b,
+           load_sem, sib_send, sib_recv,
            img_send, img_recv, txt_send, txt_recv,
            ip_send, ip_recv, tp_send, tp_recv,
            la_send, la_recv, lb_send, lb_recv):
@@ -114,10 +115,24 @@
         p = flipped(m, d)
         return copy(block(imgs, p), block(imgs, p), img_send.at[d], img_recv.at[p], image_peer(d)[1])
 
-    def text_copy(d, arriving=False):
-        p, to = text_peer(d)
-        at = p if arriving else o
-        return copy(block(txts, at), block(txts, at), txt_send.at[d], txt_recv.at[at], to)
+    even = [d for d in range(1, along) if not d & 1]
+
+    def text_copy(d):
+        return copy(block(txts, o), block(txts, o), txt_send.at[d], txt_recv.at[o], text_peer(d)[1])
+
+    def text_relay(d):
+        p = flipped(o, d)
+        return copy(block(txts, p), block(txts, p), txt_send.at[d + 1], txt_recv.at[p],
+                    text_peer(1)[1])
+
+    def text_arrival(d):
+        p = flipped(o, d)
+        return copy(block(txts, p), block(txts, p), txt_send.at[d], txt_recv.at[p], text_peer(d)[1])
+
+    def sibling_copy(d, arriving=False):
+        p = flipped(m, d if arriving else d + core)
+        return copy(block(img_part, p), sib_in.at[d], sib_send.at[d], sib_recv.at[d],
+                    image_peer(core)[1])
 
     def image_sum_copy(d, arriving=False):
         p, to = image_peer(d)
@@ -157,25 +172,28 @@
     block(imgs, m)[...] = (x * inverse_norm(x)).astype(jnp.bfloat16)
     pl.semaphore_wait(barrier, along + across - 2)
 
-    for d in range(1, along):
+    for d in even + [1] * (along > 1):
         text_copy(d).start()
-    for d in near + [core]:
+    for d in near[::-1] + [core]:
         image_copy(d).start()
     loads[2].wait()
     loads[3].wait()
     for d in near:
         image_arrival(d).wait_recv()
         image_relay(d).start()
+    for d in even:
+        text_arrival(d).wait_recv()
+        text_relay(d).start()
     for d in [core] + [d + core for d in near]:
         image_arrival(d).wait_recv()
 
     image_ids = o * wide + lax.broadcasted_iota(jnp.int32, (rows, wide), 1)
     iota = lax.broadcasted_iota(jnp.int32, (rows, wide), 0)
     loss = jnp.zeros((rows, TILE), jnp.float32)
-    for d in range(along):
+    for d in [0] + even + [d for d in range(along) if d & 1]:
         p = flipped(o, d)
-        if d:
-            text_copy(d, True).wait_recv()
+        if d & 1:
+            text_arrival(d).wait_recv()
         logits = TEMP * lax.dot_general(
             block(txts, p)[...], imgs[...], (((1,), (1,)), ((), ())),
             preferred_element_type=jnp.float32) + BIAS
@@ -204,9 +222,12 @@
 
     img_part[...] = lax.dot_general(
         coef[...], txts[...], (((0,), (0,)), ((), ())), preferred_element_type=jnp.float32)
-    for d in reversed(range(1, across)):
+    for d in near[::-1] + [0]:
+        sibling_copy(d).start()
+    for d in near[::-1]:
         p = flipped(m, d)
-        img_go[p] = pack(block(img_part, p)[...])
+        sibling_copy(d, True).wait_recv()
+        img_go[p] = pack(block(img_part, p)[...] + sib_in[d])
         image_sum_copy(d).start()
 
     for d in range(1, across):
@@ -219,7 +240,9 @@
     for d in range(1, along):
         text_sum_copy(d, True).wait_recv()
         total += unpack(txt_in[flipped(o, d)])
-    txt_out[...] = backward(txt_ref[...].astype(jnp.float32), TEMP * total)
+    txt_res[...] = backward(txt_ref[...].astype(jnp.float32), TEMP * total)
+    txt_store = pltpu.make_async_copy(txt_res, txt_out, load_sem.at[0])
+    txt_store.start()
 
     for d in range(1, along):
         loss_b_copy(d, True).wait_recv()
@@ -227,23 +250,33 @@
     open_tiles = jnp.sum((mask_v[...] == 0).astype(jnp.float32), keepdims=True)
     loss_out[...] = loss / (open_tiles * (TILE * TILE) + (loops * groups * rows))
 
-    total = block(img_part, m)[...]
-    for d in reversed(range(1, across)):
+    sibling_copy(0, True).wait_recv()
+    total = block(img_part, m)[...] + sib_in[0]
+    for d in near[::-1]:
         image_sum_copy(d, True).wait_recv()
         total += unpack(img_in[flipped(m, d)])
-    img_out[...] = backward(img_ref[...].astype(jnp.float32), TEMP * total)
+    img_res[...] = backward(img_ref[...].astype(jnp.float32), TEMP * total)
+    img_store = pltpu.make_async_copy(img_res, img_out, load_sem.at[1])
+    img_store.start()
 
     for d in near:
         image_relay(d).wait_send()
+        image_sum_copy(d).wait_send()
     for d in near + [core]:
         image_copy(d).wait_send()
+    for d in near + [0]:
+        sibling_copy(d).wait_send()
     for d in range(1, across):
-        image_sum_copy(d).wait_send()
         loss_a_copy(d).wait_send()
-    for d in range(1, along):
+    for d in even:
+        text_relay(d).wait_send()
+    for d in even + [1] * (along > 1):
         text_copy(d).wait_send()
+    for d in range(1, along):
         text_sum_copy(d).wait_send()
         loss_b_copy(d).wait_send()
+    txt_store.wait()
+    img_store.wait()
 
 
 def solution(mesh):
@@ -256,6 +289,7 @@
         wide, tall = across * rows, along * rows
         dma = pltpu.SemaphoreType.DMA
         vmem = pl.BlockSpec(memory_space=pltpu.VMEM)
+        hbm = pl.BlockSpec(memory_space=pltpu.HBM)
         image_grads, text_grads, loss = pl.pallas_call(
             functools.partial(kernel, groups, loops, inner),
             out_shape=(
@@ -263,8 +297,8 @@
                 jax.ShapeDtypeStruct((rows, width), jnp.float32),
                 jax.ShapeDtypeStruct((1, 1), jnp.float32),
             ),
-            in_specs=[pl.BlockSpec(memory_space=pltpu.HBM)] * 3,
-            out_specs=(vmem, vmem, vmem),
+            in_specs=[hbm] * 3,
+            out_specs=(hbm, hbm, vmem),
             scratch_shapes=[
                 pltpu.SMEM(tile_mask.shape, jnp.int32),
                 pltpu.VMEM(tile_mask.shape, jnp.int32),
@@ -279,12 +313,17 @@
                 pltpu.VMEM((along, rows // 2, width + 128), jnp.int32),
                 pltpu.VMEM((across, rows // 2, width + 128), jnp.int32),
                 pltpu.VMEM((along, rows // 2, width + 128), jnp.int32),
+                pltpu.VMEM((across, rows, width), jnp.float32),
+                pltpu.VMEM((rows, width), jnp.float32),
+                pltpu.VMEM((rows, width), jnp.float32),
                 pltpu.VMEM((across, 8, TILE), jnp.float32),
                 pltpu.VMEM((along, 8, TILE), jnp.float32),
                 dma((4,)),
+                dma((across,)),
+                dma((across,)),
             ] + [dma((across,)), dma((across,)), dma((along,)), dma((along,))] * 3,
             compiler_params=pltpu.CompilerParams(
-                collective_id=0, has_side_effects=True, vmem_limit_bytes=48 * 2**20),
+                collective_id=0, has_side_effects=True, vmem_limit_bytes=63_400_000),
         )(tile_mask, images, texts)
         return image_grads, text_grads, loss[0, 0]
 

time: 32.2 us -> 29.9 us (0.929)
  local copies, waits for them, and re-layouts: 3.77 us -> 2.28 us
  Pallas kernels: 25.7 us -> 24.9 us
    unnamed x8 -> x4, local copies, waits for them, and re-layouts: 3.77 us -> 2.28 us
    pallas_call x1, Pallas kernels: 25.7 us -> 24.9 us  [on_device(): pl.pallas_call(functools.partial(kernel, groups, loops, inner), out_shape...]
where the time goes in v3:
time: 29.9 us; the launch traced here: 29.7 us
  Pallas kernels  24.9 us (83%)
  between operations  2.47 us (8%)
  local copies, waits for them, and re-layouts  2.28 us (8%)
    pallas_call x1, Pallas kernels, on_device(): pl.pallas_call(functools.partial(kernel, groups, loops, inner), out_shape...  24.9 us
    unnamed x4, local copies, waits for them, and re-layouts  2.28 us

profile of v3, /device:TPU:0, one launch (start us, length us, event | category | flops | bytes accessed | tf_op | source)
XLA Modules:
  0.0 29.7 jit_solution(10246041256755355269)
XLA Ops:
  0.6 24.9 %shard_map.58 = (f32[32,1152]{1,0:T(8,128)}, f32[32,1152]{1,0:T(8,128)}, f32[1,1]{1,0:T(1,128)}) custom-call(s32[8,8]{1,0:T(8,128)} %mask_hbm.1, bf16[32,1152]{1,0:T(8,128)(2,1)} %img_hbm.1, bf16[32,1152]{1,0:T(8,128)(2,1)} %txt_hbm.1), custom_call_target="tpu_custom_call" | custom-call | tf_op jit(solution)/shard_map/pallas_call | solution.py:293
  25.6 0.0 copy-start
  25.6 1.6 %copy.9 = f32[32,1152]{1,0:T(8,128)} copy(f32[32,1152]{1,0:T(8,128)} %get-tuple-element.12) | data formatting | bytes 294912
  27.2 0.0 copy-done
  27.2 0.7 %copy.10 = f32[32,1152]{1,0:T(8,128)} copy(f32[32,1152]{1,0:T(8,128)S(1)} %copy-done) | data formatting | bytes 294912
Async XLA Ops:
  25.6 1.6 %copy-start = (f32[32,1152]{1,0:T(8,128)S(1)}, f32[32,1152]{1,0:T(8,128)}, u32[]{:S(2)}) copy-start(f32[32,1152]{1,0:T(8,128)} %get-tuple-element.13) | copy-start | bytes 442372

commit v4 on v3

--- a/solution.py
+++ b/solution.py
@@ -69,7 +69,7 @@
 def kernel(groups, loops, inner, mask_hbm, img_hbm, txt_hbm,
            img_out, txt_out, loss_out,
            mask_s, mask_v, img_ref, txt_ref,
-           imgs, txts, coef, img_part, txt_part, img_go, txt_go, img_in, txt_in, sib_in,
+           imgs, imgs_t, txts, coef, img_part, txt_part, img_go, txt_go, img_in, txt_in, sib_in,
            img_res, txt_res, loss_a, loss_b,
            load_sem, sib_send, sib_recv,
            img_send, img_recv, txt_send, txt_recv,
@@ -187,35 +187,46 @@
     for d in [core] + [d + core for d in near]:
         image_arrival(d).wait_recv()
 
+    imgs_t[...] = imgs[...].T
+    ready = [0] + even + [1] * (along > 1)
+    late = [d + 1 for d in even]
+    batches = [part[k:k + 4] for part in (ready, late) for k in range(0, len(part), 4)]
+    iota = lax.broadcasted_iota(jnp.int32, (rows, wide), 0)
     image_ids = o * wide + lax.broadcasted_iota(jnp.int32, (rows, wide), 1)
-    iota = lax.broadcasted_iota(jnp.int32, (rows, wide), 0)
     loss = jnp.zeros((rows, TILE), jnp.float32)
-    for d in [0] + even + [d for d in range(along) if d & 1]:
-        p = flipped(o, d)
-        if d & 1:
-            text_arrival(d).wait_recv()
-        logits = TEMP * lax.dot_general(
-            block(txts, p)[...], imgs[...], (((1,), (1,)), ((), ())),
+    for batch in batches:
+        places = [flipped(o, d) for d in batch]
+        for d in batch:
+            if d & 1:
+                text_arrival(d).wait_recv()
+        logits = TEMP * jnp.dot(
+            jnp.concatenate([block(txts, p)[...] for p in places], axis=0), imgs_t[...],
             preferred_element_type=jnp.float32) + BIAS
-        start = ((p * inner + i) * groups + g) * rows
-        held = jnp.concatenate([
-            jnp.full((rows, TILE), mask_s[start // TILE, (o * wide) // TILE + j], jnp.int32)
-            for j in range(wide // TILE)], axis=1)
-        matched = start + iota == image_ids
-        valid = (held == 0) | matched
+        held, matched = [], []
+        for p in places:
+            start = ((p * inner + i) * groups + g) * rows
+            held.append(jnp.concatenate([
+                jnp.full((rows, TILE), mask_s[start // TILE, (o * wide) // TILE + j], jnp.int32)
+                for j in range(wide // TILE)], axis=1))
+            matched.append((start + iota == image_ids).astype(jnp.int32))
+        matched = jnp.concatenate(matched, axis=0) != 0
+        valid = (jnp.concatenate(held, axis=0) == 0) | matched
         z = jnp.where(matched, -logits, logits)
         e = jnp.exp(-jnp.abs(logits))
         terms = jnp.where(valid, jnp.maximum(z, 0.0) + jnp.log1p(e), 0.0)
-        loss += sum(terms[:, j * TILE:(j + 1) * TILE] for j in range(wide // TILE))
+        loss += sum(terms[k * rows:(k + 1) * rows, j * TILE:(j + 1) * TILE]
+                    for k in range(len(batch)) for j in range(wide // TILE))
         sig = jnp.where(logits >= 0, 1.0, e) / (1.0 + e)
         value = jnp.where(valid, sig - matched.astype(jnp.float32), 0.0).astype(jnp.bfloat16)
-        block(coef, p)[...] = value
         sums = jnp.dot(value, imgs[...], preferred_element_type=jnp.float32)
-        if d:
-            txt_go[p] = pack(sums)
-            text_sum_copy(d).start()
-        else:
-            txt_part[...] = sums
+        for k, (d, p) in enumerate(zip(batch, places)):
+            block(coef, p)[...] = value[k * rows:(k + 1) * rows]
+            part = sums[k * rows:(k + 1) * rows]
+            if d:
+                txt_go[p] = pack(part)
+                text_sum_copy(d).start()
+            else:
+                txt_part[...] = part
     loss_a[m] = jnp.sum(loss.reshape(rows // 8, 8, TILE), axis=0)
     for d in range(1, across):
         loss_a_copy(d).start()
@@ -305,6 +316,7 @@
                 pltpu.VMEM((rows, width), jnp.bfloat16),
                 pltpu.VMEM((rows, width), jnp.bfloat16),
                 pltpu.VMEM((wide, width), jnp.bfloat16),
+                pltpu.VMEM((width, wide), jnp.bfloat16),
                 pltpu.VMEM((tall, width), jnp.bfloat16),
                 pltpu.VMEM((tall, wide), jnp.bfloat16),
                 pltpu.VMEM((wide, width), jnp.float32),
@@ -323,7 +335,7 @@
                 dma((across,)),
             ] + [dma((across,)), dma((across,)), dma((along,)), dma((along,))] * 3,
             compiler_params=pltpu.CompilerParams(
-                collective_id=0, has_side_effects=True, vmem_limit_bytes=63_400_000),
+                collective_id=0, has_side_effects=True, vmem_limit_bytes=63_192_064),
         )(tile_mask, images, texts)
         return image_grads, text_grads, loss[0, 0]
 

time: 29.9 us -> 29.6 us (0.990)
  Pallas kernels: 24.9 us -> 24.6 us
where the time goes in v4:
time: 29.6 us; the launch traced here: 29.4 us
  Pallas kernels  24.6 us (83%)
  between operations  2.47 us (8%)
  local copies, waits for them, and re-layouts  2.28 us (8%)
    pallas_call x1, Pallas kernels, on_device(): pl.pallas_call(functools.partial(kernel, groups, loops, inner), out_shape...  24.6 us
    unnamed x4, local copies, waits for them, and re-layouts  2.28 us

profile of v4, /device:TPU:0, one launch (start us, length us, event | category | flops | bytes accessed | tf_op | source)
XLA Modules:
  0.0 29.4 jit_solution(12821093333296428016)
XLA Ops:
  0.6 24.6 %shard_map.58 = (f32[32,1152]{1,0:T(8,128)}, f32[32,1152]{1,0:T(8,128)}, f32[1,1]{1,0:T(1,128)}) custom-call(s32[8,8]{1,0:T(8,128)} %mask_hbm.1, bf16[32,1152]{1,0:T(8,128)(2,1)} %img_hbm.1, bf16[32,1152]{1,0:T(8,128)(2,1)} %txt_hbm.1), custom_call_target="tpu_custom_call" | custom-call | tf_op jit(solution)/shard_map/pallas_call | solution.py:304
  25.3 0.0 copy-start
  25.3 1.6 %copy.9 = f32[32,1152]{1,0:T(8,128)} copy(f32[32,1152]{1,0:T(8,128)} %get-tuple-element.12) | data formatting | bytes 294912
  26.9 0.0 copy-done
  26.9 0.7 %copy.10 = f32[32,1152]{1,0:T(8,128)} copy(f32[32,1152]{1,0:T(8,128)S(1)} %copy-done) | data formatting | bytes 294912
Async XLA Ops:
  25.3 1.6 %copy-start = (f32[32,1152]{1,0:T(8,128)S(1)}, f32[32,1152]{1,0:T(8,128)}, u32[]{:S(2)}) copy-start(f32[32,1152]{1,0:T(8,128)} %get-tuple-element.13) | copy-start | bytes 442372

commit v5 on v4

--- a/solution.py
+++ b/solution.py
@@ -172,7 +172,7 @@
     block(imgs, m)[...] = (x * inverse_norm(x)).astype(jnp.bfloat16)
     pl.semaphore_wait(barrier, along + across - 2)
 
-    for d in even + [1] * (along > 1):
+    for d in even[::-1] + [1] * (along > 1):
         text_copy(d).start()
     for d in near[::-1] + [core]:
         image_copy(d).start()
@@ -188,8 +188,8 @@
         image_arrival(d).wait_recv()
 
     imgs_t[...] = imgs[...].T
-    ready = [0] + even + [1] * (along > 1)
-    late = [d + 1 for d in even]
+    ready = [0] + even
+    late = [d + 1 for d in ready if d + 1 < along]
     batches = [part[k:k + 4] for part in (ready, late) for k in range(0, len(part), 4)]
     iota = lax.broadcasted_iota(jnp.int32, (rows, wide), 0)
     image_ids = o * wide + lax.broadcasted_iota(jnp.int32, (rows, wide), 1)
@@ -228,13 +228,12 @@
             else:
                 txt_part[...] = part
     loss_a[m] = jnp.sum(loss.reshape(rows // 8, 8, TILE), axis=0)
-    for d in range(1, across):
-        loss_a_copy(d).start()
-
     img_part[...] = lax.dot_general(
         coef[...], txts[...], (((0,), (0,)), ((), ())), preferred_element_type=jnp.float32)
     for d in near[::-1] + [0]:
         sibling_copy(d).start()
+    for d in range(1, across):
+        loss_a_copy(d).start()
     for d in near[::-1]:
         p = flipped(m, d)
         sibling_copy(d, True).wait_recv()
@@ -288,6 +287,15 @@
         loss_b_copy(d).wait_send()
     txt_store.wait()
     img_store.wait()
+
+
+def store(first_in, second_in, first_out, second_out, sem):
+    copies = [pltpu.make_async_copy(first_in, first_out, sem.at[0]),
+              pltpu.make_async_copy(second_in, second_out, sem.at[1])]
+    for copy in copies:
+        copy.start()
+    for copy in copies:
+        copy.wait()
 
 
 def solution(mesh):
@@ -337,6 +345,14 @@
             compiler_params=pltpu.CompilerParams(
                 collective_id=0, has_side_effects=True, vmem_limit_bytes=63_192_064),
         )(tile_mask, images, texts)
+        image_grads, text_grads = pl.pallas_call(
+            store,
+            out_shape=(jax.ShapeDtypeStruct((rows, width), jnp.float32),) * 2,
+            in_specs=[hbm] * 2,
+            out_specs=(hbm, hbm),
+            scratch_shapes=[dma((2,))],
+            compiler_params=pltpu.CompilerParams(vmem_limit_bytes=63_192_064),
+        )(image_grads, text_grads)
         return image_grads, text_grads, loss[0, 0]
 
     return jax.shard_map(

time: 29.6 us -> 37 us (1.25)
  Pallas kernels: 24.6 us -> 34.4 us
  local copies, waits for them, and re-layouts: 2.28 us -> 0 us
    pallas_call x0 -> x1, Pallas kernels: none -> 10.1 us  [on_device(): pl.pallas_call(store, out_shape=(jax.ShapeDtypeStruct((rows, width), jnp....]
    unnamed x4 -> x0, local copies, waits for them, and re-layouts: 2.28 us -> none
where the time goes in v5:
time: 37 us; the launch traced here: 36.9 us
  Pallas kernels  34.4 us (93%)
  between operations  2.46 us (7%)
    pallas_call x1, Pallas kernels, on_device(): pl.pallas_call(functools.partial(kernel, groups, loops, inner), out_shape...  24.3 us
    pallas_call x1, Pallas kernels, on_device(): pl.pallas_call(store, out_shape=(jax.ShapeDtypeStruct((rows, width), jnp....  10.1 us

profile of v5, /device:TPU:0, one launch (start us, length us, event | category | flops | bytes accessed | tf_op | source)
XLA Modules:
  0.0 36.9 jit_solution(13411775926028878345)
XLA Ops:
  0.6 24.3 %shard_map.58 = (f32[32,1152]{1,0:T(8,128)}, f32[32,1152]{1,0:T(8,128)}, f32[1,1]{1,0:T(1,128)}) custom-call(s32[8,8]{1,0:T(8,128)} %mask_hbm.1, bf16[32,1152]{1,0:T(8,128)(2,1)} %img_hbm.1, bf16[32,1152]{1,0:T(8,128)(2,1)} %txt_hbm.1), custom_call_target="tpu_custom_call" | custom-call | tf_op jit(solution)/shard_map/pallas_call | solution.py:312
  25.0 10.1 %shard_map.59 = (f32[32,1152]{1,0:T(8,128)}, f32[32,1152]{1,0:T(8,128)}) custom-call(f32[32,1152]{1,0:T(8,128)} %get-tuple-element.8.first_in, f32[32,1152]{1,0:T(8,128)} %get-tuple-element.9.second_in), custom_call_target="tpu_custom_call" | custom-call | tf_op jit(solution)/shard_map/pallas_call | solution.py:348

commit v6 on v4

--- a/solution.py
+++ b/solution.py
@@ -11,6 +11,7 @@
 TEMP = 10.0
 BIAS = -2.0
 EPS = 1e-06
+PARTS = 2
 LOG_2 = 0.6931471805599453
 MESH = pl.DeviceIdType.MESH
 
@@ -64,6 +65,23 @@
     fixed = jnp.concatenate([lax.shift_right_arithmetic(words, 16), low], axis=0).astype(jnp.float32)
     width = fixed.shape[1] - 128
     return fixed[:, :width] * step_of(fixed[:, width:width + 1])
+
+
+class Copies:
+    def __init__(self, parts):
+        self.parts = parts
+
+    def start(self):
+        for part in self.parts:
+            part.start()
+
+    def wait_send(self):
+        for part in self.parts:
+            part.wait_send()
+
+    def wait_recv(self):
+        for part in self.parts:
+            part.wait_recv()
 
 
 def kernel(groups, loops, inner, mask_hbm, img_hbm, txt_hbm,
@@ -96,10 +114,12 @@
     def block(ref, p):
         return ref.at[pl.ds(pl.multiple_of(p * rows, rows), rows)]
 
-    def copy(src, dst, send, recv, to):
-        return pltpu.make_async_remote_copy(
-            src_ref=src, dst_ref=dst, send_sem=send, recv_sem=recv,
-            device_id=to, device_id_type=MESH)
+    def copy(src, dst, send, recv, to, parts=PARTS):
+        size = src.shape[0] // parts
+        return Copies([pltpu.make_async_remote_copy(
+            src_ref=src.at[pl.ds(k * size, size)], dst_ref=dst.at[pl.ds(k * size, size)],
+            send_sem=send.at[k], recv_sem=recv.at[k],
+            device_id=to, device_id_type=MESH) for k in range(parts)])
 
     near = [d for d in range(1, across) if not d & core]
 
@@ -147,12 +167,12 @@
     def loss_a_copy(d, arriving=False):
         p, to = image_peer(d)
         at = p if arriving else m
-        return copy(loss_a.at[m], loss_a.at[at], la_send.at[d], la_recv.at[at], to)
+        return copy(loss_a.at[m], loss_a.at[at], la_send.at[d], la_recv.at[at], to, 1)
 
     def loss_b_copy(d, arriving=False):
         p, to = text_peer(d)
         at = p if arriving else o
-        return copy(loss_b.at[o], loss_b.at[at], lb_send.at[d], lb_recv.at[at], to)
+        return copy(loss_b.at[o], loss_b.at[at], lb_send.at[d], lb_recv.at[at], to, 1)
 
     loads = [pltpu.make_async_copy(src, dst, load_sem.at[k]) for k, (src, dst) in enumerate(
         [(txt_hbm, txt_ref), (img_hbm, img_ref), (mask_hbm, mask_s), (mask_hbm, mask_v)])]
@@ -172,24 +192,26 @@
     block(imgs, m)[...] = (x * inverse_norm(x)).astype(jnp.bfloat16)
     pl.semaphore_wait(barrier, along + across - 2)
 
-    for d in even + [1] * (along > 1):
+    for d in even[::-1] + [1] * (along > 1):
         text_copy(d).start()
     for d in near[::-1] + [core]:
         image_copy(d).start()
     loads[2].wait()
     loads[3].wait()
     for d in near:
-        image_arrival(d).wait_recv()
-        image_relay(d).start()
+        for part, relay in zip(image_arrival(d).parts, image_relay(d).parts):
+            part.wait_recv()
+            relay.start()
     for d in even:
-        text_arrival(d).wait_recv()
-        text_relay(d).start()
+        for part, relay in zip(text_arrival(d).parts, text_relay(d).parts):
+            part.wait_recv()
+            relay.start()
     for d in [core] + [d + core for d in near]:
         image_arrival(d).wait_recv()
 
     imgs_t[...] = imgs[...].T
-    ready = [0] + even + [1] * (along > 1)
-    late = [d + 1 for d in even]
+    ready = [0] + even
+    late = [d + 1 for d in ready if d + 1 < along]
     batches = [part[k:k + 4] for part in (ready, late) for k in range(0, len(part), 4)]
     iota = lax.broadcasted_iota(jnp.int32, (rows, wide), 0)
     image_ids = o * wide + lax.broadcasted_iota(jnp.int32, (rows, wide), 1)
@@ -228,13 +250,12 @@
             else:
                 txt_part[...] = part
     loss_a[m] = jnp.sum(loss.reshape(rows // 8, 8, TILE), axis=0)
-    for d in range(1, across):
-        loss_a_copy(d).start()
-
     img_part[...] = lax.dot_general(
         coef[...], txts[...], (((0,), (0,)), ((), ())), preferred_element_type=jnp.float32)
     for d in near[::-1] + [0]:
         sibling_copy(d).start()
+    for d in range(1, across):
+        loss_a_copy(d).start()
     for d in near[::-1]:
         p = flipped(m, d)
         sibling_copy(d, True).wait_recv()
@@ -331,11 +352,11 @@
                 pltpu.VMEM((across, 8, TILE), jnp.float32),
                 pltpu.VMEM((along, 8, TILE), jnp.float32),
                 dma((4,)),
-                dma((across,)),
-                dma((across,)),
-            ] + [dma((across,)), dma((across,)), dma((along,)), dma((along,))] * 3,
+                dma((across, PARTS)),
+                dma((across, PARTS)),
+            ] + [dma((across, PARTS)), dma((across, PARTS)), dma((along, PARTS)), dma((along, PARTS))] * 3,
             compiler_params=pltpu.CompilerParams(
-                collective_id=0, has_side_effects=True, vmem_limit_bytes=63_192_064),
+                collective_id=0, has_side_effects=True, vmem_limit_bytes=63_123_000),
         )(tile_mask, images, texts)
         return image_grads, text_grads, loss[0, 0]
 

time: 29.6 us -> 30.1 us (1.017)
  Pallas kernels: 24.6 us -> 25.2 us
    pallas_call x1, Pallas kernels: 24.6 us -> 25.2 us  [on_device(): pl.pallas_call(functools.partial(kernel, groups, loops, inner), out_shape...]
where the time goes in v6:
time: 30.1 us; the launch traced here: 29.9 us
  Pallas kernels  25.2 us (84%)
  between operations  2.47 us (8%)
  local copies, waits for them, and re-layouts  2.28 us (8%)
    pallas_call x1, Pallas kernels, on_device(): pl.pallas_call(functools.partial(kernel, groups, loops, inner), out_shape...  25.2 us
    unnamed x4, local copies, waits for them, and re-layouts  2.28 us

profile of v6, /device:TPU:0, one launch (start us, length us, event | category | flops | bytes accessed | tf_op | source)
XLA Modules:
  0.0 29.9 jit_solution(6196244347978876194)
XLA Ops:
  0.6 25.2 %shard_map.58 = (f32[32,1152]{1,0:T(8,128)}, f32[32,1152]{1,0:T(8,128)}, f32[1,1]{1,0:T(1,128)}) custom-call(s32[8,8]{1,0:T(8,128)} %mask_hbm.1, bf16[32,1152]{1,0:T(8,128)(2,1)} %img_hbm.1, bf16[32,1152]{1,0:T(8,128)(2,1)} %txt_hbm.1), custom_call_target="tpu_custom_call" | custom-call | tf_op jit(solution)/shard_map/pallas_call | solution.py:325
  25.8 0.0 copy-start
  25.8 1.6 %copy.9 = f32[32,1152]{1,0:T(8,128)} copy(f32[32,1152]{1,0:T(8,128)} %get-tuple-element.12) | data formatting | bytes 294912
  27.4 0.0 copy-done
  27.4 0.7 %copy.10 = f32[32,1152]{1,0:T(8,128)} copy(f32[32,1152]{1,0:T(8,128)S(1)} %copy-done) | data formatting | bytes 294912
Async XLA Ops:
  25.8 1.6 %copy-start = (f32[32,1152]{1,0:T(8,128)S(1)}, f32[32,1152]{1,0:T(8,128)}, u32[]{:S(2)}) copy-start(f32[32,1152]{1,0:T(8,128)} %get-tuple-element.13) | copy-start | bytes 442372

commit v7 on v4

--- a/solution.py
+++ b/solution.py
@@ -172,7 +172,7 @@
     block(imgs, m)[...] = (x * inverse_norm(x)).astype(jnp.bfloat16)
     pl.semaphore_wait(barrier, along + across - 2)
 
-    for d in even + [1] * (along > 1):
+    for d in even[::-1] + [1] * (along > 1):
         text_copy(d).start()
     for d in near[::-1] + [core]:
         image_copy(d).start()
@@ -188,12 +188,23 @@
         image_arrival(d).wait_recv()
 
     imgs_t[...] = imgs[...].T
-    ready = [0] + even + [1] * (along > 1)
-    late = [d + 1 for d in even]
+    ready = [0] + even
+    late = [d + 1 for d in ready if d + 1 < along]
     batches = [part[k:k + 4] for part in (ready, late) for k in range(0, len(part), 4)]
     iota = lax.broadcasted_iota(jnp.int32, (rows, wide), 0)
     image_ids = o * wide + lax.broadcasted_iota(jnp.int32, (rows, wide), 1)
     loss = jnp.zeros((rows, TILE), jnp.float32)
+
+    def send_text_sums(batch, value):
+        sums = jnp.dot(value, imgs[...], preferred_element_type=jnp.float32)
+        for k, d in enumerate(batch):
+            part = sums[k * rows:(k + 1) * rows]
+            if d:
+                txt_go[flipped(o, d)] = pack(part)
+                text_sum_copy(d).start()
+            else:
+                txt_part[...] = part
+
     for batch in batches:
         places = [flipped(o, d) for d in batch]
         for d in batch:
@@ -218,23 +229,24 @@
                     for k in range(len(batch)) for j in range(wide // TILE))
         sig = jnp.where(logits >= 0, 1.0, e) / (1.0 + e)
         value = jnp.where(valid, sig - matched.astype(jnp.float32), 0.0).astype(jnp.bfloat16)
-        sums = jnp.dot(value, imgs[...], preferred_element_type=jnp.float32)
-        for k, (d, p) in enumerate(zip(batch, places)):
+        for k, p in enumerate(places):
             block(coef, p)[...] = value[k * rows:(k + 1) * rows]
-            part = sums[k * rows:(k + 1) * rows]
-            if d:
-                txt_go[p] = pack(part)
-                text_sum_copy(d).start()
-            else:
-                txt_part[...] = part
+        if batch is not batches[-1]:
+            send_text_sums(batch, value)
     loss_a[m] = jnp.sum(loss.reshape(rows // 8, 8, TILE), axis=0)
+    half = across // 2
+    for far in (1, 0):
+        at = flipped(m, far * half) // half * half * rows
+        at = pl.multiple_of(at, half * rows)
+        img_part[pl.ds(at, half * rows)] = lax.dot_general(
+            coef[:, pl.ds(at, half * rows)], txts[...], (((0,), (0,)), ((), ())),
+            preferred_element_type=jnp.float32)
+        for d in near[::-1] + [0]:
+            if (d >= half) == bool(far):
+                sibling_copy(d).start()
+    send_text_sums(batches[-1], value)
     for d in range(1, across):
         loss_a_copy(d).start()
-
-    img_part[...] = lax.dot_general(
-        coef[...], txts[...], (((0,), (0,)), ((), ())), preferred_element_type=jnp.float32)
-    for d in near[::-1] + [0]:
-        sibling_copy(d).start()
     for d in near[::-1]:
         p = flipped(m, d)
         sibling_copy(d, True).wait_recv()
@@ -254,12 +266,6 @@
     txt_res[...] = backward(txt_ref[...].astype(jnp.float32), TEMP * total)
     txt_store = pltpu.make_async_copy(txt_res, txt_out, load_sem.at[0])
     txt_store.start()
-
-    for d in range(1, along):
-        loss_b_copy(d, True).wait_recv()
-    loss = jnp.sum(jnp.sum(loss_b[...], axis=0), keepdims=True)
-    open_tiles = jnp.sum((mask_v[...] == 0).astype(jnp.float32), keepdims=True)
-    loss_out[...] = loss / (open_tiles * (TILE * TILE) + (loops * groups * rows))
 
     sibling_copy(0, True).wait_recv()
     total = block(img_part, m)[...] + sib_in[0]
@@ -269,6 +275,12 @@
     img_res[...] = backward(img_ref[...].astype(jnp.float32), TEMP * total)
     img_store = pltpu.make_async_copy(img_res, img_out, load_sem.at[1])
     img_store.start()
+
+    for d in range(1, along):
+        loss_b_copy(d, True).wait_recv()
+    loss = jnp.sum(jnp.sum(loss_b[...], axis=0), keepdims=True)
+    open_tiles = jnp.sum((mask_v[...] == 0).astype(jnp.float32), keepdims=True)
+    loss_out[...] = loss / (open_tiles * (TILE * TILE) + (loops * groups * rows))
 
     for d in near:
         image_relay(d).wait_send()

time: 29.6 us -> 28.6 us (0.966)
  Pallas kernels: 24.6 us -> 23.7 us
    pallas_call x1, Pallas kernels: 24.6 us -> 23.7 us  [on_device(): pl.pallas_call(functools.partial(kernel, groups, loops, inner), out_shape...]
where the time goes in v7:
time: 28.6 us; the launch traced here: 28.4 us
  Pallas kernels  23.7 us (83%)
  between operations  2.47 us (9%)
  local copies, waits for them, and re-layouts  2.28 us (8%)
    pallas_call x1, Pallas kernels, on_device(): pl.pallas_call(functools.partial(kernel, groups, loops, inner), out_shape...  23.7 us
    unnamed x4, local copies, waits for them, and re-layouts  2.28 us

profile of v7, /device:TPU:0, one launch (start us, length us, event | category | flops | bytes accessed | tf_op | source)
XLA Modules:
  0.0 28.4 jit_solution(10854932220643623167)
XLA Ops:
  0.6 23.7 %shard_map.58 = (f32[32,1152]{1,0:T(8,128)}, f32[32,1152]{1,0:T(8,128)}, f32[1,1]{1,0:T(1,128)}) custom-call(s32[8,8]{1,0:T(8,128)} %mask_hbm.1, bf16[32,1152]{1,0:T(8,128)(2,1)} %img_hbm.1, bf16[32,1152]{1,0:T(8,128)(2,1)} %txt_hbm.1), custom_call_target="tpu_custom_call" | custom-call | tf_op jit(solution)/shard_map/pallas_call | solution.py:316
  24.3 0.0 copy-start
  24.3 1.6 %copy.9 = f32[32,1152]{1,0:T(8,128)} copy(f32[32,1152]{1,0:T(8,128)} %get-tuple-element.12) | data formatting | bytes 294912
  26.0 0.0 copy-done
  26.0 0.7 %copy.10 = f32[32,1152]{1,0:T(8,128)} copy(f32[32,1152]{1,0:T(8,128)S(1)} %copy-done) | data formatting | bytes 294912
Async XLA Ops:
  24.3 1.6 %copy-start = (f32[32,1152]{1,0:T(8,128)S(1)}, f32[32,1152]{1,0:T(8,128)}, u32[]{:S(2)}) copy-start(f32[32,1152]{1,0:T(8,128)} %get-tuple-element.13) | copy-start | bytes 442372

commit v8 on v7

--- a/solution.py
+++ b/solution.py
@@ -66,16 +66,16 @@
     return fixed[:, :width] * step_of(fixed[:, width:width + 1])
 
 
-def kernel(groups, loops, inner, mask_hbm, img_hbm, txt_hbm,
+def kernel(groups, loops, inner, mask_s, both_ref,
            img_out, txt_out, loss_out,
-           mask_s, mask_v, img_ref, txt_ref,
            imgs, imgs_t, txts, coef, img_part, txt_part, img_go, txt_go, img_in, txt_in, sib_in,
-           img_res, txt_res, loss_a, loss_b,
-           load_sem, sib_send, sib_recv,
+           loss_a, loss_b,
+           sib_send, sib_recv,
            img_send, img_recv, txt_send, txt_recv,
            ip_send, ip_recv, tp_send, tp_recv,
            la_send, la_recv, lb_send, lb_recv):
-    rows = img_ref.shape[0]
+    rows = both_ref.shape[0] // 2
+    img_ref, txt_ref = both_ref.at[pl.ds(0, rows)], both_ref.at[pl.ds(rows, rows)]
     across = groups * inner
     along = loops // inner
     g = lax.axis_index("grp")
@@ -154,20 +154,14 @@
         at = p if arriving else o
         return copy(loss_b.at[o], loss_b.at[at], lb_send.at[d], lb_recv.at[at], to)
 
-    loads = [pltpu.make_async_copy(src, dst, load_sem.at[k]) for k, (src, dst) in enumerate(
-        [(txt_hbm, txt_ref), (img_hbm, img_ref), (mask_hbm, mask_s), (mask_hbm, mask_v)])]
-    for load in loads:
-        load.start()
     barrier = pltpu.get_barrier_semaphore()
     for d in range(1, along):
         pl.semaphore_signal(barrier, inc=1, device_id=text_peer(d)[1], device_id_type=MESH)
     for d in range(1, across):
         pl.semaphore_signal(barrier, inc=1, device_id=image_peer(d)[1], device_id_type=MESH)
 
-    loads[0].wait()
     x = txt_ref[...].astype(jnp.float32)
     block(txts, o)[...] = (x * inverse_norm(x)).astype(jnp.bfloat16)
-    loads[1].wait()
     x = img_ref[...].astype(jnp.float32)
     block(imgs, m)[...] = (x * inverse_norm(x)).astype(jnp.bfloat16)
     pl.semaphore_wait(barrier, along + across - 2)
@@ -176,8 +170,6 @@
         text_copy(d).start()
     for d in near[::-1] + [core]:
         image_copy(d).start()
-    loads[2].wait()
-    loads[3].wait()
     for d in near:
         image_arrival(d).wait_recv()
         image_relay(d).start()
@@ -194,6 +186,7 @@
     iota = lax.broadcasted_iota(jnp.int32, (rows, wide), 0)
     image_ids = o * wide + lax.broadcasted_iota(jnp.int32, (rows, wide), 1)
     loss = jnp.zeros((rows, TILE), jnp.float32)
+    open_tiles = jnp.int32(0)
 
     def send_text_sums(batch, value):
         sums = jnp.dot(value, imgs[...], preferred_element_type=jnp.float32)
@@ -216,9 +209,10 @@
         held, matched = [], []
         for p in places:
             start = ((p * inner + i) * groups + g) * rows
-            held.append(jnp.concatenate([
-                jnp.full((rows, TILE), mask_s[start // TILE, (o * wide) // TILE + j], jnp.int32)
-                for j in range(wide // TILE)], axis=1))
+            marks = [mask_s[start // TILE, (o * wide) // TILE + j] for j in range(wide // TILE)]
+            open_tiles += sum(jnp.where(mark == 0, 1, 0) for mark in marks)
+            held.append(jnp.concatenate(
+                [jnp.full((rows, TILE), mark, jnp.int32) for mark in marks], axis=1))
             matched.append((start + iota == image_ids).astype(jnp.int32))
         matched = jnp.concatenate(matched, axis=0) != 0
         valid = (jnp.concatenate(held, axis=0) == 0) | matched
@@ -233,7 +227,8 @@
             block(coef, p)[...] = value[k * rows:(k + 1) * rows]
         if batch is not batches[-1]:
             send_text_sums(batch, value)
-    loss_a[m] = jnp.sum(loss.reshape(rows // 8, 8, TILE), axis=0)
+    loss_a[m, 0:8] = jnp.sum(loss.reshape(rows // 8, 8, TILE), axis=0)
+    loss_a[m, 8:16] = jnp.full((8, TILE), open_tiles * (rows * TILE), jnp.int32).astype(jnp.float32)
     half = across // 2
     for far in (1, 0):
         at = flipped(m, far * half) // half * half * rows
@@ -263,24 +258,19 @@
     for d in range(1, along):
         text_sum_copy(d, True).wait_recv()
         total += unpack(txt_in[flipped(o, d)])
-    txt_res[...] = backward(txt_ref[...].astype(jnp.float32), TEMP * total)
-    txt_store = pltpu.make_async_copy(txt_res, txt_out, load_sem.at[0])
-    txt_store.start()
+    txt_out[...] = backward(txt_ref[...].astype(jnp.float32), TEMP * total)
 
     sibling_copy(0, True).wait_recv()
     total = block(img_part, m)[...] + sib_in[0]
     for d in near[::-1]:
         image_sum_copy(d, True).wait_recv()
         total += unpack(img_in[flipped(m, d)])
-    img_res[...] = backward(img_ref[...].astype(jnp.float32), TEMP * total)
-    img_store = pltpu.make_async_copy(img_res, img_out, load_sem.at[1])
-    img_store.start()
+    img_out[...] = backward(img_ref[...].astype(jnp.float32), TEMP * total)
 
     for d in range(1, along):
         loss_b_copy(d, True).wait_recv()
-    loss = jnp.sum(jnp.sum(loss_b[...], axis=0), keepdims=True)
-    open_tiles = jnp.sum((mask_v[...] == 0).astype(jnp.float32), keepdims=True)
-    loss_out[...] = loss / (open_tiles * (TILE * TILE) + (loops * groups * rows))
+    total = jnp.sum(loss_b[...], axis=0)
+    loss_out[...] = jnp.sum(total[0:8], keepdims=True) / (total[8:9, 0:1] + (loops * groups * rows))
 
     for d in near:
         image_relay(d).wait_send()
@@ -298,8 +288,6 @@
     for d in range(1, along):
         text_sum_copy(d).wait_send()
         loss_b_copy(d).wait_send()
-    txt_store.wait()
-    img_store.wait()
 
 
 def solution(mesh):
@@ -312,7 +300,6 @@
         wide, tall = across * rows, along * rows
         dma = pltpu.SemaphoreType.DMA
         vmem = pl.BlockSpec(memory_space=pltpu.VMEM)
-        hbm = pl.BlockSpec(memory_space=pltpu.HBM)
         image_grads, text_grads, loss = pl.pallas_call(
             functools.partial(kernel, groups, loops, inner),
             out_shape=(
@@ -320,13 +307,9 @@
                 jax.ShapeDtypeStruct((rows, width), jnp.float32),
                 jax.ShapeDtypeStruct((1, 1), jnp.float32),
             ),
-            in_specs=[hbm] * 3,
-            out_specs=(hbm, hbm, vmem),
+            in_specs=[pl.BlockSpec(memory_space=pltpu.SMEM), vmem],
+            out_specs=(vmem, vmem, vmem),
             scratch_shapes=[
-                pltpu.SMEM(tile_mask.shape, jnp.int32),
-                pltpu.VMEM(tile_mask.shape, jnp.int32),
-                pltpu.VMEM((rows, width), jnp.bfloat16),
-                pltpu.VMEM((rows, width), jnp.bfloat16),
                 pltpu.VMEM((wide, width), jnp.bfloat16),
                 pltpu.VMEM((width, wide), jnp.bfloat16),
                 pltpu.VMEM((tall, width), jnp.bfloat16),
@@ -338,17 +321,14 @@
                 pltpu.VMEM((across, rows // 2, width + 128), jnp.int32),
                 pltpu.VMEM((along, rows // 2, width + 128), jnp.int32),
                 pltpu.VMEM((across, rows, width), jnp.float32),
-                pltpu.VMEM((rows, width), jnp.float32),
-                pltpu.VMEM((rows, width), jnp.float32),
-                pltpu.VMEM((across, 8, TILE), jnp.float32),
-                pltpu.VMEM((along, 8, TILE), jnp.float32),
-                dma((4,)),
+                pltpu.VMEM((across, 16, TILE), jnp.float32),
+                pltpu.VMEM((along, 16, TILE), jnp.float32),
                 dma((across,)),
                 dma((across,)),
             ] + [dma((across,)), dma((across,)), dma((along,)), dma((along,))] * 3,
             compiler_params=pltpu.CompilerParams(
-                collective_id=0, has_side_effects=True, vmem_limit_bytes=63_192_064),
-        )(tile_mask, images, texts)
+                collective_id=0, has_side_effects=True, vmem_limit_bytes=48 * 2**20),
+        )(tile_mask, jnp.concatenate([images, texts], axis=0))
         return image_grads, text_grads, loss[0, 0]
 
     return jax.shard_map(

time: 28.6 us -> 29.3 us (1.024); the launches traced: 28.4 us -> 28.8 us
  local copies, waits for them, and re-layouts: 2.28 us -> 1.33 us
  other arithmetic: 0 us -> 0.94 us
  Pallas kernels: 23.7 us -> 24.1 us
    unnamed x4, local copies, waits for them, and re-layouts: 2.28 us -> 1.33 us
    concatenate x0 -> x1, other arithmetic: none -> 0.94 us  [on_device(): jnp.concatenate([images, texts], axis=0)]
    pallas_call x1, Pallas kernels: 23.7 us -> 24.1 us  [on_device(): pl.pallas_call(functools.partial(kernel, groups, loops, inner), out_shape...]
where the time goes in v8:
time: 29.3 us; the launch traced here: 28.8 us
  Pallas kernels  24.1 us (82%)
  between operations  2.42 us (8%)
  local copies, waits for them, and re-layouts  1.33 us (5%)
  other arithmetic  0.94 us (3%)
    pallas_call x1, Pallas kernels, on_device(): pl.pallas_call(functools.partial(kernel, groups, loops, inner), out_shape...  24.1 us
    unnamed x4, local copies, waits for them, and re-layouts  1.33 us
    concatenate x1, other arithmetic, on_device(): jnp.concatenate([images, texts], axis=0)  0.94 us

profile of v8, /device:TPU:0, one launch (start us, length us, event | category | flops | bytes accessed | tf_op | source)
XLA Modules:
  0.0 28.8 jit_solution(3823468568430380158)
XLA Ops:
  0.6 0.0 copy-start
  0.6 0.9 %pad_maximum_fusion.both_ref = bf16[64,1152]{1,0:T(8,128)(2,1)S(1)} fusion(bf16[32,1152]{1,0:T(8,128)(2,1)} %param.4, bf16[32,1152]{1,0:T(8,128)(2,1)} %param.3), kind=kLoop, calls=%fused_computation | loop fusion | flops 294912 | bytes 294912 | tf_op jit(solution)/shard_map/concatenate | solution.py:331
  1.6 0.0 copy-done
  1.6 24.1 %shard_map.58 = (f32[32,1152]{1,0:T(8,128)S(1)}, f32[32,1152]{1,0:T(8,128)S(1)}, f32[1,1]{1,0:T(1,128)}) custom-call(s32[8,8]{1,0:T(8,128)S(1)} %copy-done, bf16[64,1152]{1,0:T(8,128)(2,1)S(1)} %pad_maximum_fusion.both_ref), custom_call_target="tpu_custom_call" | custom-call | tf_op jit(solution)/shard_map/pallas_call | solution.py:303
  25.7 0.7 %copy.9 = f32[32,1152]{1,0:T(8,128)} copy(f32[32,1152]{1,0:T(8,128)S(1)} %get-tuple-element.12) | data formatting | bytes 294912
  26.3 0.7 %copy.10 = f32[32,1152]{1,0:T(8,128)} copy(f32[32,1152]{1,0:T(8,128)S(1)} %get-tuple-element.13) | data formatting | bytes 294912
Async XLA Ops:
  0.6 1.0 %copy-start = (s32[8,8]{1,0:T(8,128)S(1)}, s32[8,8]{1,0:T(8,128)}, u32[]{:S(2)}) copy-start(s32[8,8]{1,0:T(8,128)} %mask_s.1) | copy-start | bytes 772

commit v9 on v7

--- a/solution.py
+++ b/solution.py
@@ -178,12 +178,15 @@
         image_copy(d).start()
     loads[2].wait()
     loads[3].wait()
-    for d in near:
+    for d in near[:1]:
         image_arrival(d).wait_recv()
         image_relay(d).start()
     for d in even:
         text_arrival(d).wait_recv()
         text_relay(d).start()
+    for d in near[1:]:
+        image_arrival(d).wait_recv()
+        image_relay(d).start()
     for d in [core] + [d + core for d in near]:
         image_arrival(d).wait_recv()
 

time: 28.6 us -> 28.6 us (level)
  no operation moved by 1% of the time
where the time goes in v9:
time: 28.6 us; the launch traced here: 28.4 us
  Pallas kernels  23.7 us (83%)
  between operations  2.47 us (9%)
  local copies, waits for them, and re-layouts  2.28 us (8%)
    pallas_call x1, Pallas kernels, on_device(): pl.pallas_call(functools.partial(kernel, groups, loops, inner), out_shape...  23.7 us
    unnamed x4, local copies, waits for them, and re-layouts  2.28 us

profile of v9, /device:TPU:0, one launch (start us, length us, event | category | flops | bytes accessed | tf_op | source)
XLA Modules:
  0.0 28.4 jit_solution(16263541718062906804)
XLA Ops:
  0.6 23.7 %shard_map.58 = (f32[32,1152]{1,0:T(8,128)}, f32[32,1152]{1,0:T(8,128)}, f32[1,1]{1,0:T(1,128)}) custom-call(s32[8,8]{1,0:T(8,128)} %mask_hbm.1, bf16[32,1152]{1,0:T(8,128)(2,1)} %img_hbm.1, bf16[32,1152]{1,0:T(8,128)(2,1)} %txt_hbm.1), custom_call_target="tpu_custom_call" | custom-call | tf_op jit(solution)/shard_map/pallas_call | solution.py:319
  24.3 0.0 copy-start
  24.3 1.6 %copy.9 = f32[32,1152]{1,0:T(8,128)} copy(f32[32,1152]{1,0:T(8,128)} %get-tuple-element.12) | data formatting | bytes 294912
  26.0 0.0 copy-done
  26.0 0.7 %copy.10 = f32[32,1152]{1,0:T(8,128)} copy(f32[32,1152]{1,0:T(8,128)S(1)} %copy-done) | data formatting | bytes 294912
Async XLA Ops:
  24.3 1.6 %copy-start = (f32[32,1152]{1,0:T(8,128)S(1)}, f32[32,1152]{1,0:T(8,128)}, u32[]{:S(2)}) copy-start(f32[32,1152]{1,0:T(8,128)} %get-tuple-element.13) | copy-start | bytes 442372

commit v10 on v7

--- a/solution.py
+++ b/solution.py
@@ -347,7 +347,7 @@
                 dma((across,)),
             ] + [dma((across,)), dma((across,)), dma((along,)), dma((along,))] * 3,
             compiler_params=pltpu.CompilerParams(
-                collective_id=0, has_side_effects=True, vmem_limit_bytes=63_192_064),
+                collective_id=0, has_side_effects=True, vmem_limit_bytes=62_900_000),
         )(tile_mask, images, texts)
         return image_grads, text_grads, loss[0, 0]
 

time: 28.6 us -> 28.6 us (level)
  no operation moved by 1% of the time
where the time goes in v10:
time: 28.6 us; the launch traced here: 28.4 us
  Pallas kernels  23.7 us (83%)
  between operations  2.47 us (9%)
  local copies, waits for them, and re-layouts  2.28 us (8%)
    pallas_call x1, Pallas kernels, on_device(): pl.pallas_call(functools.partial(kernel, groups, loops, inner), out_shape...  23.7 us
    unnamed x4, local copies, waits for them, and re-layouts  2.28 us

profile of v10, /device:TPU:0, one launch (start us, length us, event | category | flops | bytes accessed | tf_op | source)
XLA Modules:
  0.0 28.4 jit_solution(10854932220643623167)
XLA Ops:
  0.6 23.7 %shard_map.58 = (f32[32,1152]{1,0:T(8,128)}, f32[32,1152]{1,0:T(8,128)}, f32[1,1]{1,0:T(1,128)}) custom-call(s32[8,8]{1,0:T(8,128)} %mask_hbm.1, bf16[32,1152]{1,0:T(8,128)(2,1)} %img_hbm.1, bf16[32,1152]{1,0:T(8,128)(2,1)} %txt_hbm.1), custom_call_target="tpu_custom_call" | custom-call | tf_op jit(solution)/shard_map/pallas_call | solution.py:316
  24.3 0.0 copy-start
  24.3 1.6 %copy.9 = f32[32,1152]{1,0:T(8,128)} copy(f32[32,1152]{1,0:T(8,128)} %get-tuple-element.12) | data formatting | bytes 294912
  26.0 0.0 copy-done
  26.0 0.7 %copy.10 = f32[32,1152]{1,0:T(8,128)} copy(f32[32,1152]{1,0:T(8,128)S(1)} %copy-done) | data formatting | bytes 294912
Async XLA Ops:
  24.3 1.6 %copy-start = (f32[32,1152]{1,0:T(8,128)S(1)}, f32[32,1152]{1,0:T(8,128)}, u32[]{:S(2)}) copy-start(f32[32,1152]{1,0:T(8,128)} %get-tuple-element.13) | copy-start | bytes 442372
